TPU v7x, 256 devices: a whole 4x4x8 slice. The times are simulated.
256 devices in a mesh: ctx: 32 (over x, y, core), tp: 4 (over z_lo), sec: 2 (over z_hi).
Axes of the slice: x: 4, y: 4, z: 8 (z_hi: 2, z_lo: 4; z = z_hi * 4 + z_lo), core: 2. Of those that a mesh axis runs over, the one named last changes fastest.
Arguments:
- queries: bfloat16 [2, 2048, 8192], P('sec', 'ctx', 'tp'), may hold values from -16 to 16
- keys: bfloat16 [2, 2048, 1024], P('sec', 'ctx', 'tp'), may hold values from -6 to 6
- values: bfloat16 [2, 2048, 1024], P('sec', 'ctx', 'tp'), may hold values from -24 to 24
- page_owner: int32 [256, 2], replicated, may hold values from 0 to 31, all different within a row; in each aligned block of 8 rows (0 to 7, 8 to 15, ...) at most 2 rows name the same one
- lengths: int32 [32, 16], P('ctx'), may hold values from 1 to 512, 3968 in all within a row
- page_table: int32 [32, 512], P('ctx'), may hold values from 0 to 511, as said below
- group_cache_keys: bfloat16 [16384, 8, 1024], P('ctx', None, 'tp'), may hold values from -6 to 6
- group_cache_values: bfloat16 [16384, 8, 1024], P('ctx', None, 'tp'), may hold values from -24 to 24
Outputs:
- attended: bfloat16 [2, 2048, 8192], P('sec', 'ctx', 'tp')
Inputs may be any that keep to these rules, and one draw needn't show every extreme that they name: `page_owner`: each row names 2 different decode groups; within the 8 rows of one prompt index no group is named more than 2 times. Each group's 16 lengths sum to 3968 and the largest of them is 512. `page_table`: each row names every page of 0 to 511 once.
All inputs are finite; a program needn't handle non-finite values.
Results may differ from a plain program's by a relative error of at most 0.0034.
Values may be sent and summed in bfloat16 or wider, within the bound.
No kernel may reach another device: no remote copies, remote signals or barrier semaphores. Data moves between devices by JAX's collectives and lax.ppermute only.
A program may use at most 64 MiB of HBM per device.

v0:
```python
import math

import jax
import jax.numpy as jnp
from jax import lax
from jax.sharding import PartitionSpec as P

HEAD_WIDTH = 128
DECODE_STEPS = 4
PAGE_TOKENS = 8
TOP = 2
MAXP = 64


def shifted(shard, axis, by):
    count = lax.axis_size(axis)
    pairs = [(i, i + by) for i in range(count) if 0 <= i + by < count]
    return lax.ppermute(shard, axis, pairs)


def body(
    queries, keys, values, page_owner, lengths, page_table, group_cache_keys, group_cache_values
):
    section = lax.axis_index("sec")
    is_prefill = section == 0
    cycle_size = lax.axis_size("ctx")
    cycle_place = lax.axis_index("ctx")
    fresh_q = queries[0]
    fresh_k = keys[0]
    fresh_v = values[0]
    count_of_rows = fresh_q.shape[0]
    width_kv = fresh_k.shape[1]
    width_q = fresh_q.shape[1]
    heads_kv = width_kv // HEAD_WIDTH
    group_width = width_q // width_kv
    score_scale = HEAD_WIDTH ** (-0.5)
    own_base = cycle_place * count_of_rows
    lay_rows = fresh_q.shape[0]
    lay_ids = jnp.arange(lay_rows, dtype=jnp.int32)
    lay_pos = own_base + lay_ids
    work_rows = fresh_q.shape[0]
    state_now = (
        jnp.full((heads_kv, group_width, work_rows), -1e30, jnp.float32),
        jnp.zeros((heads_kv, group_width, work_rows), jnp.float32),
        jnp.zeros((heads_kv, group_width, work_rows, HEAD_WIDTH), jnp.float32),
    )
    k_piece = lax.all_gather(fresh_k, "ctx", axis=0, tiled=True)
    v_piece = lax.all_gather(fresh_v, "ctx", axis=0, tiled=True)
    key_count = k_piece.shape[0]
    heads = k_piece.shape[1] // HEAD_WIDTH
    absorb_work_rows = fresh_q.shape[0]
    query_heads = fresh_q.reshape(absorb_work_rows, heads, group_width, HEAD_WIDTH)
    last_pos = jnp.max(lay_pos)
    key_pos = jnp.arange(key_count, dtype=jnp.int32)

    def update(state_in):
        run_max, run_sum, run_acc = state_in
        scores = (
            jnp.einsum(
                "nkgd,mkd->kgnm",
                query_heads,
                k_piece.reshape(key_count, heads, HEAD_WIDTH),
                preferred_element_type=jnp.float32,
            )
            * score_scale
        )
        allowed = key_pos[None, :] <= lay_pos[:, None]
        scores = jnp.where(allowed, scores, -1e30)
        next_max = jnp.maximum(run_max, jnp.max(scores, axis=-1))
        weights = jnp.where(allowed, jnp.exp(scores - next_max[..., None]), 0.0)
        next_sum = jnp.sum(weights, axis=-1)
        next_acc = jnp.einsum(
            "kgnm,mkd->kgnd",
            weights.astype(jnp.bfloat16),
            v_piece.reshape(key_count, heads, HEAD_WIDTH),
            preferred_element_type=jnp.float32,
        )
        return (next_max, next_sum, next_acc)

    def keep(state_in):
        return state_in

    state_end = lax.cond(is_prefill & (jnp.int32(0) <= last_pos), update, keep, state_now)
    run_max, run_sum, run_acc = state_end
    heads = run_acc.shape[0]
    work_rows = run_acc.shape[2]
    safe_sum = jnp.where(run_sum > 0, run_sum, 1.0)
    result = (run_acc / safe_sum[..., None]).transpose(2, 0, 1, 3)
    lay_out = result.reshape(work_rows, heads * group_width * HEAD_WIDTH).astype(jnp.bfloat16)
    pages_dev = count_of_rows // PAGE_TOKENS
    item_count = pages_dev * TOP
    cap_slots = max(2, 2 * item_count // cycle_size)
    hand_slots = cycle_size * cap_slots
    own_routes = lax.dynamic_slice_in_dim(
        page_owner, cycle_place * pages_dev, pages_dev, 0
    ).reshape(item_count)
    group_ids = jnp.arange(cycle_size, dtype=jnp.int32)
    dest_hits = (own_routes[:, None] == group_ids[None, :]).astype(jnp.int32)
    before = jnp.cumsum(dest_hits, axis=0) - dest_hits
    slot_index = own_routes * cap_slots + jnp.sum(before * dest_hits, axis=1)
    slot_hits = (slot_index[:, None] == jnp.arange(hand_slots, dtype=jnp.int32)[None, :]).astype(
        jnp.bfloat16
    )
    page_hits = (
        (jnp.arange(item_count, dtype=jnp.int32) // TOP)[:, None]
        == jnp.arange(pages_dev, dtype=jnp.int32)[None, :]
    ).astype(jnp.bfloat16)
    placing = jnp.dot(slot_hits.T, page_hits, preferred_element_type=jnp.float32).astype(
        jnp.bfloat16
    )
    both_pages = jnp.stack([fresh_k, fresh_v]).reshape(2, pages_dev, PAGE_TOKENS * width_kv)
    outgoing = jnp.einsum("hp,spc->shc", placing, both_pages, preferred_element_type=jnp.float32)
    outgoing = outgoing.astype(jnp.bfloat16).reshape(
        2, cycle_size, cap_slots, PAGE_TOKENS, width_kv
    )
    spread_out = lax.all_to_all(outgoing, "ctx", split_axis=1, concat_axis=1, tiled=True)
    arrived = shifted(spread_out, "sec", 1)
    arrived = arrived.reshape(2, hand_slots, PAGE_TOKENS, width_kv)
    all_routes = page_owner.reshape(cycle_size, item_count)
    arrivals = jnp.sum((all_routes == cycle_place).astype(jnp.int32), axis=1)
    filled = (jnp.arange(cap_slots, dtype=jnp.int32)[None, :] < arrivals[:, None]).reshape(
        hand_slots
    )
    fill_mask = filled[:, None, None]
    new_keys = jnp.concatenate(
        [
            jnp.where(fill_mask, arrived[0], group_cache_keys[:hand_slots]),
            group_cache_keys[hand_slots:],
        ],
        axis=0,
    )
    new_values = jnp.concatenate(
        [
            jnp.where(fill_mask, arrived[1], group_cache_values[:hand_slots]),
            group_cache_values[hand_slots:],
        ],
        axis=0,
    )
    sequence_count = count_of_rows // DECODE_STEPS
    pool_count = page_table.shape[1]
    needed = (lengths + PAGE_TOKENS - 1) // PAGE_TOKENS
    offsets = jnp.cumsum(needed, axis=1) - needed
    wanted = offsets[:, :, None] + jnp.arange(MAXP, dtype=jnp.int32)[None, None, :]
    wanted = jnp.minimum(wanted, pool_count - 1)
    slot_table = jnp.take_along_axis(page_table, wanted.reshape(1, sequence_count * MAXP), axis=1)
    slot_table = slot_table.reshape(sequence_count, MAXP)
    block_seqs = math.gcd(sequence_count, 8)
    block_count = sequence_count // block_seqs

    def run_decode(pools):
        cached_key_rows, cached_value_rows = pools
        q_blocks = queries[1].reshape(
            block_count, block_seqs, DECODE_STEPS, heads_kv, group_width, HEAD_WIDTH
        )
        k_blocks = keys[1].reshape(block_count, block_seqs, DECODE_STEPS, heads_kv, HEAD_WIDTH)
        v_blocks = values[1].reshape(block_count, block_seqs, DECODE_STEPS, heads_kv, HEAD_WIDTH)
        len_blocks = lengths.reshape(block_count, block_seqs)
        table_blocks = slot_table.reshape(block_count, block_seqs, MAXP)
        step_pos = jnp.arange(DECODE_STEPS, dtype=jnp.int32)
        causal = (step_pos[None, :] <= step_pos[:, None])[None, None, None]

        def one_block(pieces):
            q_part, k_part, v_part, len_part, table_part = pieces
            previous_key = cached_key_rows[table_part].reshape(
                block_seqs, MAXP * PAGE_TOKENS, heads_kv, HEAD_WIDTH
            )
            previous_value = cached_value_rows[table_part].reshape(
                block_seqs, MAXP * PAGE_TOKENS, heads_kv, HEAD_WIDTH
            )
            cache_pos = jnp.arange(MAXP * PAGE_TOKENS, dtype=jnp.int32)
            live_mask = (cache_pos[None, :] < len_part[:, None])[:, None, None, None, :]
            old_scores = (
                jnp.einsum(
                    "bsjgd,bljd->bjgsl", q_part, previous_key, preferred_element_type=jnp.float32
                )
                * score_scale
            )
            old_scores = jnp.where(live_mask, old_scores, -1e30)
            new_scores = (
                jnp.einsum("bsjgd,btjd->bjgst", q_part, k_part, preferred_element_type=jnp.float32)
                * score_scale
            )
            new_scores = jnp.where(causal, new_scores, -1e30)
            row_peak = jnp.maximum(jnp.max(old_scores, axis=-1), jnp.max(new_scores, axis=-1))[
                ..., None
            ]
            old_weights = jnp.where(live_mask, jnp.exp(old_scores - row_peak), 0.0)
            new_weights = jnp.where(causal, jnp.exp(new_scores - row_peak), 0.0)
            totals = jnp.sum(old_weights, axis=-1) + jnp.sum(new_weights, axis=-1)
            mixed_sum = jnp.einsum(
                "bjgsl,bljd->bjgsd",
                old_weights.astype(jnp.bfloat16),
                previous_value,
                preferred_element_type=jnp.float32,
            )
            mixed_sum = mixed_sum + jnp.einsum(
                "bjgst,btjd->bjgsd",
                new_weights.astype(jnp.bfloat16),
                v_part,
                preferred_element_type=jnp.float32,
            )
            result = (mixed_sum / totals[..., None]).transpose(0, 3, 1, 2, 4)
            return result.reshape(block_seqs * DECODE_STEPS, heads_kv * group_width * HEAD_WIDTH)

        block_out = lax.map(one_block, (q_blocks, k_blocks, v_blocks, len_blocks, table_blocks))
        return block_out.reshape(count_of_rows, heads_kv * group_width * HEAD_WIDTH).astype(
            jnp.bfloat16
        )

    def skip_decode(pools):
        return jnp.zeros(fresh_q.shape, jnp.bfloat16)

    decode_out = lax.cond(is_prefill, skip_decode, run_decode, (new_keys, new_values))
    return jnp.where(is_prefill, lay_out, decode_out)[None]


def solution(mesh):
    return jax.shard_map(
        body,
        mesh=mesh,
        in_specs=(
            P("sec", "ctx", "tp"),
            P("sec", "ctx", "tp"),
            P("sec", "ctx", "tp"),
            P(),
            P("ctx", None),
            P("ctx", None),
            P("ctx", None, "tp"),
            P("ctx", None, "tp"),
        ),
        out_specs=P("sec", "ctx", "tp"),
        check_vma=False,
    )
```

profile of v0, /device:TPU:1, one launch (start us, length us, event | category | flops | bytes accessed | tf_op | source)
XLA Modules:
  0.0 135.5 jit_solution(17878019733101213837)
XLA Ops:
  6.5 0.0 copy-start.12
  6.5 0.0 all-gather.5.cloned.1.call-start
  6.5 0.7 all-gather.5.cloned.1.call-update
  7.3 0.8 constant_dynamic-slice_fusion.4
  8.0 0.1 copy.38
  8.1 0.1 reshape.329
  8.2 0.1 fusion.61
  8.3 0.8 pad_maximum_fusion.2
  9.1 0.2 select_reduce_fusion
  9.3 0.6 convolution_convert_fusion
  9.9 0.1 copy.60
  10.0 0.9 copy.39
  10.9 8.6 %all-to-all-start = ((bf16[2,32,2,8,256]{4,3,2,0,1:T(8,128)(2,1)}), bf16[2,32,2,8,256]{4,3,2,0,1:T(8,128)(2,1)S(1)}, u32[]{:S(2)}, u32[]{:S(2)}) async-start(bf16[2,32,2,8,256]{4,3,2,0,1:T(8,128)(2,1)} %copy.39), calls=%async_computation | async-start | bytes 1048576 | tf_op jit(solution)/shard_map/all_to_all | solution.py:116
  19.5 0.0 all-gather.7.cloned.1.call-start
  19.5 0.7 all-gather.7.cloned.1.call-update
  20.2 0.0 copy-done.13
  20.3 0.2 reduce_window_sum.22
  20.5 0.1 add.167
  20.5 0.1 add.174
  20.6 0.1 add.168
  20.7 0.0 copy-done.12
  20.7 0.1 reduce_sum.53
  20.8 0.1 reduce_sum.54
  20.9 0.1 iota_compare_fusion.2
  21.0 0.1 lt.98
  21.1 0.0 copy-start.2
  21.2 0.1 add.176
  21.2 0.1 add.170
  21.3 0.6 fusion.67
  22.6 8.5 %all-to-all-done = bf16[2,32,2,8,256]{4,3,2,0,1:T(8,128)(2,1)S(1)} async-done(((bf16[2,32,2,8,256]{4,3,2,0,1:T(8,128)(2,1)}), bf16[2,32,2,8,256]{4,3,2,0,1:T(8,128)(2,1)S(1)}, u32[]{:S(2)}, u32[]{:S(2)}) %all-to-all-start) | async-done | bytes 524320 | tf_op jit(solution)/shard_map/all_to_all | solution.py:116
  31.1 9.0 %collective-permute-start = (bf16[2,32,2,8,256]{4,3,2,0,1:T(8,128)(2,1)S(1)}, bf16[2,32,2,8,256]{4,3,2,0,1:T(8,128)(2,1)S(1)}, u32[]{:S(2)}, u32[]{:S(2)}) collective-permute-start(bf16[2,32,2,8,256]{4,3,2,0,1:T(8,128)(2,1)S(1)} %all-to-all-done), channel_id=1, source_target_pairs={{0,1},{2,3},{4,5},{6,7},{8,9},{10,11},{12,13},{14,15},{16,17},{18,... | collective-permute-start | bytes 1572872 | tf_op jit(solution)/shard_map/ppermute | solution.py:18
  40.1 0.5 iota_add_fusion
  40.6 10.9 %collective-permute-done = bf16[2,32,2,8,256]{4,3,2,0,1:T(8,128)(2,1)S(1)} collective-permute-done((bf16[2,32,2,8,256]{4,3,2,0,1:T(8,128)(2,1)S(1)}, bf16[2,32,2,8,256]{4,3,2,0,1:T(8,128)(2,1)S(1)}, u32[]{:S(2)}, u32[]{:S(2)}) %collective-permute-start) | collective-permute-done | bytes 524320 | tf_op jit(solution)/shard_map/ppermute | solution.py:18
  51.5 0.0 copy-done.2
  51.6 1.1 bitcast_select_fusion.2
  52.7 0.0 slice-done.1
  52.7 0.0 slice-start
  52.7 1.5 %pad_maximum_fusion.1 = bf16[512,8,256]{2,1,0:T(8,128)(2,1)} fusion(bf16[448,8,256]{2,1,0:T(8,128)(2,1)S(1)} %slice-done.1, bf16[64,8,256]{2,1,0:T(8,128)(2,1)S(1)} %get-tuple-element.217), kind=kLoop, calls=%fused_computation.70 | loop fusion | flops 1048576 | bytes 4194304 | tf_op jit(solution)/shard_map/concatenate | solution.py:132
  54.2 0.8 slice-done
  55.0 1.5 %pad_maximum_fusion = bf16[512,8,256]{2,1,0:T(8,128)(2,1)} fusion(bf16[448,8,256]{2,1,0:T(8,128)(2,1)S(1)} %slice-done, bf16[64,8,256]{2,1,0:T(8,128)(2,1)S(1)} %get-tuple-element.218), kind=kLoop, calls=%fused_computation.69 | loop fusion | flops 1048576 | bytes 4194304 | tf_op jit(solution)/shard_map/concatenate | solution.py:125
  56.5 0.0 copy-done
  56.5 0.0 copy-done.4
  56.5 0.0 copy-done.6
  56.5 0.0 copy-done.7
  56.5 0.7 conditional.3
  56.6 0.7 broadcast.267
  57.3 4.7 %all-gather.5.cloned.1.call-done = bf16[1,2048,256]{2,1,0:T(8,128)(2,1)} async-done(((bf16[1,64,256]{2,1,0:T(8,128)(2,1)}), bf16[1,2048,256]{2,1,0:T(8,128)(2,1)}) %all-gather.5.cloned.1.call-update) | async-done | bytes 1048592 | tf_op jit(solution)/shard_map/all_gather | solution.py:47
  62.0 49.8 %all-gather.7.cloned.1.call-done = bf16[1,2048,256]{2,1,0:T(8,128)(2,1)} async-done(((bf16[1,64,256]{2,1,0:T(8,128)(2,1)}), bf16[1,2048,256]{2,1,0:T(8,128)(2,1)}) %all-gather.7.cloned.1.call-update) | async-done | bytes 1048592 | tf_op jit(solution)/shard_map/all_gather | solution.py:48
  111.8 15.7 %conditional.2 = (f32[2,8,64]{2,1,0:T(8,128)S(1)}, f32[2,8,64,128]{3,2,1,0:T(8,128)S(1)}) conditional(s32[]{:T(128)} %convert_element_type.48, () %tuple.23, (s32[2048]{0:T(1024)S(1)}, s32[64]{0:T(128)}, bf16[2048,256]{1,0:T(8,128)(2,1)}, bf16[1,64,2048]{2,1,0:T(8,128)(2,1)}, bf16[2048,256]{1,0:T(8,128)(2,1)}) %tuple.69), branch_computations={%region_1.0_spmd, %region_2.5_spmd} | conditional | flops 1101134848 | bytes 72122720 | solution.py:83
  111.8 0.8 broadcast_compare_fusion
  112.6 1.3 reshape.320
  113.9 0.0 copy-done.5
  114.0 0.0 copy-start.3
  114.0 4.8 %fusion.2 = (f32[2,8,64]{2,1,0:T(8,128)S(1)}, f32[2,2048,64,8]{1,2,3,0:T(8,128)}) fusion(pred[64,2048]{1,0:T(8,128)(4,1)S(1)} %broadcast_compare_fusion, bf16[64,2,8,128]{3,2,1,0:T(8,128)(2,1)S(1)} %bitcast.131, bf16[2048,2,128,1]{2,1,0,3:T(2,128)(2,1)S(1)} %bitcast.128), kind=kOutput, calls=%fused_computation.6 | convolution fusion | flops 543161344 | bytes 9834496 | tf_op jit(solution)/shard_map/cond/branch_1_fun/nkgd,mkd->kgnm/dot_general | solution.py:59
  118.8 0.0 copy-done.3
  118.8 0.3 reshape.321
  119.1 0.0 copy-start.1
  119.1 5.3 %fusion.5 = f32[2,8,64,128]{3,2,1,0:T(8,128)S(1)} fusion(f32[2,2048,64,8]{1,2,3,0:T(8,128)} %get-tuple-element.208, f32[2,8,64]{2,1,0:T(8,128)S(1)} %broadcast_maximum_fusion, pred[64,2048]{1,0:T(8,128)(4,1)S(1)} %broadcast_compare_fusion, bf16[2048,2,128,1]{2,1,0,3:T(2,128)(2,1)S(1)} %bitcast.134), kind=kOutput, calls=%fused_computation.9 | convolution fusion | flops 547356672 | bytes 10096640 | tf_op jit(solution)/shard_map/cond/branch_1_fun/kgnm,mkd->kgnd/dot_general | solution.py:72
  124.4 0.5 copy-done.1
  124.9 2.6 %fusion.4 = f32[2,8,64]{2,1,0:T(8,128)S(1)} fusion(f32[2,2048,64,8]{1,2,3,0:T(8,128)S(1)} %copy-done.1, f32[2,8,64]{2,1,0:T(8,128)S(1)} %broadcast_maximum_fusion, pred[64,2048]{1,0:T(8,128)(4,1)S(1)} %broadcast_compare_fusion), kind=kLoop, calls=%fused_computation.8 | loop fusion | flops 10484736 | bytes 8527872 | tf_op jit(solution)/shard_map/cond/branch_1_fun/reduce_sum | solution.py:71
  127.5 0.2 fusion.60
  127.7 0.2 copy.37
  127.9 0.0 copy-done.11
  127.9 0.8 fusion.59
  (25 shorter events, 0.2 us)
Async XLA Ops:
  6.5 14.2 %copy-start.12 = (s32[256,2]{0,1:T(2,128)S(1)}, s32[256,2]{0,1:T(2,128)}, u32[]{:S(2)}) copy-start(s32[256,2]{0,1:T(2,128)} %param.17) | copy-start | bytes 6148
  6.5 13.7 %copy-start.13 = (s32[1,16]{1,0:T(1,128)S(1)}, s32[1,16]{1,0:T(1,128)}, u32[]{:S(2)}) copy-start(s32[1,16]{1,0:T(1,128)} %param.18) | copy-start | bytes 196
  6.5 55.4 %all-gather.5.cloned.1.call-start = ((), (), s32[]{:S(2)}) async-start(), calls=%async_computation.1 | async-start | bytes 1081344 | tf_op jit(solution)/shard_map/all_gather | solution.py:47
  10.9 20.2 %all-to-all-start = ((bf16[2,32,2,8,256]{4,3,2,0,1:T(8,128)(2,1)}), bf16[2,32,2,8,256]{4,3,2,0,1:T(8,128)(2,1)S(1)}, u32[]{:S(2)}, u32[]{:S(2)}) async-start(bf16[2,32,2,8,256]{4,3,2,0,1:T(8,128)(2,1)} %copy.39), calls=%async_computation | async-start | bytes 1048576 | tf_op jit(solution)/shard_map/all_to_all | solution.py:116
  19.5 92.3 %all-gather.7.cloned.1.call-start = ((), (), s32[]{:S(2)}) async-start(), calls=%async_computation.2 | async-start | bytes 1081344 | tf_op jit(solution)/shard_map/all_gather | solution.py:48
  21.1 30.4 %copy-start.2 = (bf16[512,8,256]{2,1,0:T(8,128)(2,1)S(1)}, bf16[512,8,256]{2,1,0:T(8,128)(2,1)}, u32[]{:S(2)}) copy-start(bf16[512,8,256]{2,1,0:T(8,128)(2,1)} %param.20) | copy-start | bytes 6291460
  31.1 21.6 %slice-start.1 = ((bf16[512,8,256]{2,1,0:T(8,128)(2,1)}), bf16[448,8,256]{2,1,0:T(8,128)(2,1)S(1)}, s32[]{:S(2)}) async-start(bf16[512,8,256]{2,1,0:T(8,128)(2,1)} %param.21), calls=%async_computation.4 | async-start | bytes 3670016 | tf_op jit(solution)/shard_map/slice | solution.py:135
  31.1 20.4 %collective-permute-start = (bf16[2,32,2,8,256]{4,3,2,0,1:T(8,128)(2,1)S(1)}, bf16[2,32,2,8,256]{4,3,2,0,1:T(8,128)(2,1)S(1)}, u32[]{:S(2)}, u32[]{:S(2)}) collective-permute-start(bf16[2,32,2,8,256]{4,3,2,0,1:T(8,128)(2,1)S(1)} %all-to-all-done), channel_id=1, source_target_pairs={{0,1},{2,3},{4,5},{6,7},{8,9},{10,11},{12,13},{14,15},{16,17},{18,... | collective-permute-start | bytes 1572872 | tf_op jit(solution)/shard_map/ppermute | solution.py:18
  52.7 2.3 %slice-start = ((bf16[512,8,256]{2,1,0:T(8,128)(2,1)}), bf16[448,8,256]{2,1,0:T(8,128)(2,1)S(1)}, s32[]{:S(2)}) async-start(bf16[512,8,256]{2,1,0:T(8,128)(2,1)} %param.20), calls=%async_computation.3 | async-start | bytes 3670016 | tf_op jit(solution)/shard_map/slice | solution.py:128
  54.9 1.6 %copy-start = (s32[1,512]{1,0:T(1,128)S(1)}, s32[1,512]{1,0:T(1,128)}, u32[]{:S(2)}) copy-start(s32[1,512]{1,0:T(1,128)} %param.19) | copy-start | bytes 6148
  54.9 1.6 %copy-start.4 = (bf16[1,64,2048]{2,1,0:T(8,128)(2,1)S(1)}, bf16[1,64,2048]{2,1,0:T(8,128)(2,1)}, u32[]{:S(2)}) copy-start(bf16[1,64,2048]{2,1,0:T(8,128)(2,1)} %param.14) | copy-start | bytes 786436
  54.9 1.6 %copy-start.6 = (bf16[1,64,256]{2,1,0:T(8,128)(2,1)S(1)}, bf16[1,64,256]{2,1,0:T(8,128)(2,1)}, u32[]{:S(2)}) copy-start(bf16[1,64,256]{2,1,0:T(8,128)(2,1)} %param.15) | copy-start | bytes 98308
  54.9 1.6 %copy-start.7 = (bf16[1,64,256]{2,1,0:T(8,128)(2,1)S(1)}, bf16[1,64,256]{2,1,0:T(8,128)(2,1)}, u32[]{:S(2)}) copy-start(bf16[1,64,256]{2,1,0:T(8,128)(2,1)} %param.16) | copy-start | bytes 98308
  111.8 16.1 %copy-start.11 = (bf16[64,2048]{1,0:T(8,128)(2,1)S(1)}, bf16[64,2048]{1,0:T(8,128)(2,1)}, u32[]{:S(2)}) copy-start(bf16[64,2048]{1,0:T(8,128)(2,1)} %get-tuple-element.322) | copy-start | bytes 786436
  111.8 2.1 %copy-start.5 = (bf16[1,64,2048]{2,1,0:T(8,128)(2,1)S(1)}, bf16[1,64,2048]{2,1,0:T(8,128)(2,1)}, u32[]{:S(2)}) copy-start(bf16[1,64,2048]{2,1,0:T(8,128)(2,1)} %get-tuple-element.78) | copy-start | bytes 786436 | tf_op jit(solution)/shard_map/cond
  114.0 4.8 %copy-start.3 = (bf16[2048,256]{1,0:T(8,128)(2,1)S(1)}, bf16[2048,256]{1,0:T(8,128)(2,1)}, u32[]{:S(2)}) copy-start(bf16[2048,256]{1,0:T(8,128)(2,1)} %get-tuple-element.79) | copy-start | bytes 3145732 | tf_op jit(solution)/shard_map/cond
  119.1 5.8 %copy-start.1 = (f32[2,2048,64,8]{1,2,3,0:T(8,128)S(1)}, f32[2,2048,64,8]{1,2,3,0:T(8,128)}, u32[]{:S(2)}) copy-start(f32[2,2048,64,8]{1,2,3,0:T(8,128)} %get-tuple-element.208) | copy-start | bytes 25165828 | tf_op jit(solution)/shard_map/cond
Sparse Core Ops, SparseCore 0:
  9.9 52.0 all-gather.4
  64.5 47.2 all-gather.6
where the time goes:
time: 136 us
  waiting for transfers between devices  75.3 us (55%)
  starting transfers between devices  17.6 us (13%)
  between operations  14.2 us (10%)
  other arithmetic  11.1 us (8%)
  matrix products  10.8 us (8%)
  local copies, waits for them, and re-layouts  6.43 us (5%)
    all_gather x1, waiting for transfers between devices, body(): v_piece = lax.all_gather(fresh_v, 'ctx', axis=0, tiled=True)  49.8 us
    ppermute x1, waiting for transfers between devices, shifted(): return lax.ppermute(shard, axis, pairs)  10.9 us
    ppermute x1, starting transfers between devices, shifted(): return lax.ppermute(shard, axis, pairs)  8.97 us
    all_to_all x1, starting transfers between devices, body(): lax.all_to_all(outgoing, 'ctx', split_axis=1, concat_axis=1, tiled=True)  8.59 us
    all_to_all x1, waiting for transfers between devices, body(): lax.all_to_all(outgoing, 'ctx', split_axis=1, concat_axis=1, tiled=True)  8.5 us
    dot_general x1, matrix products, update(): jnp.einsum('kgnm,mkd->kgnd', weights.astype(jnp.bfloat16), v_piece.reshap...  5.33 us
    dot_general x1, matrix products, update(): jnp.einsum('nkgd,mkd->kgnm', query_heads, k_piece.reshape(key_count, head...  4.82 us
    all_gather x1, waiting for transfers between devices, body(): k_piece = lax.all_gather(fresh_k, 'ctx', axis=0, tiled=True)  4.71 us
  transfers between devices with their start and end apart: 4, of which 4 were waited for; matrix products, arithmetic and copies ran while one was open for 8% of the time, Pallas kernels for 0%

commit v1 on v0

v1 whole, which is shorter than its diff:
```python
import math

import jax
import jax.numpy as jnp
import numpy as np
from jax import lax
from jax.experimental import pallas as pl
from jax.experimental.pallas import tpu as pltpu
from jax.sharding import Mesh
from jax.sharding import PartitionSpec as P

HEAD_WIDTH = 128
GROUP_WIDTH = 8
KV_HEADS = 2
ROWS = 64
QROWS = GROUP_WIDTH * ROWS
WIDTH = KV_HEADS * HEAD_WIDTH
PAGE_TOKENS = 8
PAGES = 512
HAND = 64
SEQS = 16
STEPS = 4
TOP = 2
PPD = 8
TOKENS = PAGES * PAGE_TOKENS
HAND_TOKENS = HAND * PAGE_TOKENS
CHUNK = 256
BIG = float(2**20)
TO_LOG2 = HEAD_WIDTH**-0.5 * math.log2(math.e)
SIDE = 4
AXES = ("x", "y", "c", "t", "s")
SIZES = {"x": 4, "y": 4, "c": 2, "t": 4, "s": 2}
CTX = ("x", "y", "c")
VMEM_LIMIT = 48 * 1024 * 1024
F32 = jnp.float32
BF16 = jnp.bfloat16
I32 = jnp.int32


def moved(shard, axes, target):
    sizes = [SIZES[a] for a in axes]
    pairs = []
    for source in range(math.prod(sizes)):
        place = [int(i) for i in np.unravel_index(source, sizes)]
        goal = target(*place)
        if goal is not None:
            goal = [a % b for a, b in zip(goal, sizes)]
            pairs.append((source, int(np.ravel_multi_index(goal, sizes))))
    return lax.ppermute(shard, axes if len(axes) > 1 else axes[0], pairs)


def iota(shape, axis):
    return lax.broadcasted_iota(I32, shape, axis)


def fill_queries(q_ref, qa_ref):
    hot = jnp.where(iota((QROWS, 128), 0) % ROWS == iota((QROWS, 128), 1), 1.0, 0.0).astype(BF16)
    for j in range(KV_HEADS):
        for h in range(GROUP_WIDTH):
            at = (j * GROUP_WIDTH + h) * HEAD_WIDTH
            qa_ref[j, h * ROWS : (h + 1) * ROWS, 0:HEAD_WIDTH] = q_ref[:, at : at + HEAD_WIDTH]
        qa_ref[j, :, HEAD_WIDTH:] = hot


def head_lanes(j):
    return pl.ds(pl.multiple_of(j * HEAD_WIDTH, HEAD_WIDTH), HEAD_WIDTH)


def attend(j, qa_ref, count, key_of, value_of, bias_of, s_ref, mx_ref, m_ref, acc_ref, first):
    mx_ref[...] = jnp.full((QROWS, 128), -4.0 * BIG, F32) if first else m_ref[j]

    def scores(c, carry):
        keys = jnp.concatenate([key_of(c, j), bias_of(c)], axis=1)
        s = lax.dot_general(
            qa_ref[j], keys, (((1,), (1,)), ((), ())), preferred_element_type=F32
        )
        s_ref[c] = s
        mx_ref[...] = jnp.maximum(mx_ref[...], jnp.maximum(s[:, :128], s[:, 128:]))
        return carry

    lax.fori_loop(0, count, scores, 0)
    top = jnp.broadcast_to(jnp.max(mx_ref[...], axis=1, keepdims=True), (QROWS, 128))
    if first:
        acc_ref[j] = jnp.zeros((QROWS, 2 * HEAD_WIDTH), F32)
    else:
        shrink = jnp.exp2((m_ref[j] - top) * TO_LOG2)
        acc_ref[j] = acc_ref[j] * jnp.concatenate([shrink, shrink], axis=1)
    m_ref[j] = top
    ones = jnp.ones((CHUNK, HEAD_WIDTH), BF16)

    def mix(c, carry):
        low = m_ref[j]
        weights = jnp.exp2((s_ref[c] - jnp.concatenate([low, low], axis=1)) * TO_LOG2)
        wide = jnp.concatenate([value_of(c, j), ones], axis=1)
        acc_ref[j] += jnp.dot(weights.astype(BF16), wide, preferred_element_type=F32)
        return carry

    lax.fori_loop(0, count, mix, 0)


def finish(acc_ref, out_ref):
    for j in range(KV_HEADS):
        result = (acc_ref[j, :, :HEAD_WIDTH] / acc_ref[j, :, HEAD_WIDTH:]).astype(BF16)
        for h in range(GROUP_WIDTH):
            at = (j * GROUP_WIDTH + h) * HEAD_WIDTH
            out_ref[:, at : at + HEAD_WIDTH] = result[h * ROWS : (h + 1) * ROWS]


def place():
    return lax.axis_index("x"), lax.axis_index("y"), lax.axis_index("c")


def prompt_bias(block, me):
    key_pos = block * ROWS + iota((ROWS, 128), 0)
    row_pos = me * ROWS + iota((ROWS, 128), 1)
    return jnp.where(key_pos > row_pos, -BIG, 0.0).astype(BF16)


def prompt_kernel(pieces, first, last, info_ref, q_ref, *refs):
    count = len(pieces)
    piece_refs, refs = refs[:count], refs[count:]
    if not first:
        m_in, acc_in, refs = refs[0], refs[1], refs[2:]
    if last:
        out_ref, m_ref, acc_ref = refs[0], refs[-2], refs[-1]
        refs = refs[1:-2]
    else:
        m_ref, acc_ref, refs = refs[0], refs[1], refs[2:]
    kv_ref, bias_ref, s_ref, mx_ref, qa_ref, sems = refs
    copies = [
        pltpu.make_async_copy(ref, kv_ref.at[i], sems.at[i]) for i, ref in enumerate(piece_refs)
    ]
    for copy in copies:
        copy.start()
    x, y, c = info_ref[0], info_ref[1], info_ref[2]
    me = x * 8 + y * 2 + c
    for i, (swapped, k2) in enumerate(pieces):
        core = (1 - c) if swapped else c
        for k1 in range(SIDE):
            on_x = jnp.where(core == 0, k2, k1)
            on_y = jnp.where(core == 0, k1, k2)
            block = ((x - on_x) & 3) * 8 + ((y - on_y) & 3) * 2 + core
            bias_ref[i, k1 * ROWS : (k1 + 1) * ROWS, :] = prompt_bias(block, me)
    fill_queries(q_ref, qa_ref)
    if not first:
        m_ref[...] = m_in[...]
        acc_ref[...] = acc_in[...]
    for copy in copies:
        copy.wait()

    def key_of(i, j):
        return kv_ref[i, :, 0, :, head_lanes(j)].reshape(CHUNK, HEAD_WIDTH)

    def value_of(i, j):
        return kv_ref[i, :, 1, :, head_lanes(j)].reshape(CHUNK, HEAD_WIDTH)

    def one_head(j, carry):
        attend(
            j, qa_ref, count, key_of, value_of, lambda i: bias_ref[i],
            s_ref, mx_ref, m_ref, acc_ref, first,
        )
        return carry

    lax.fori_loop(0, KV_HEADS, one_head, 0)
    if last:
        finish(acc_ref, out_ref)


STATE = [
    jax.ShapeDtypeStruct((KV_HEADS, QROWS, 128), F32),
    jax.ShapeDtypeStruct((KV_HEADS, QROWS, 2 * HEAD_WIDTH), F32),
]


def vmem():
    return pl.BlockSpec(memory_space=pltpu.VMEM)


def prompt_attend(info, q, arrays, pieces, state, last):
    count = len(pieces)
    first = state is None
    scratch = [
        pltpu.VMEM((count, SIDE, 2, ROWS, WIDTH), BF16),
        pltpu.VMEM((count, CHUNK, 128), BF16),
        pltpu.VMEM((count, QROWS, CHUNK), F32),
        pltpu.VMEM((QROWS, 128), F32),
        pltpu.VMEM((KV_HEADS, QROWS, 2 * HEAD_WIDTH), BF16),
        pltpu.SemaphoreType.DMA((count,)),
    ]
    if last:
        scratch += [pltpu.VMEM(s.shape, s.dtype) for s in STATE]
    keys = count * CHUNK

    def kernel(*refs):
        prompt_kernel(pieces, first, last, *refs)

    return pl.pallas_call(
        kernel,
        out_shape=jax.ShapeDtypeStruct((ROWS, q.shape[1]), BF16) if last else STATE,
        in_specs=[pl.BlockSpec(memory_space=pltpu.SMEM), vmem()]
        + [pl.BlockSpec(memory_space=pl.ANY)] * count
        + ([] if first else [vmem(), vmem()]),
        out_specs=vmem() if last else [vmem(), vmem()],
        scratch_shapes=scratch,
        compiler_params=pltpu.CompilerParams(vmem_limit_bytes=VMEM_LIMIT),
        cost_estimate=pl.CostEstimate(
            flops=4 * KV_HEADS * QROWS * keys * 256,
            bytes_accessed=keys * WIDTH * 4,
            transcendentals=KV_HEADS * QROWS * keys,
        ),
    )(info, q, *arrays, *(() if first else state))


POOL_CHUNKS = TOKENS // CHUNK + 1


def pool_kernel(
    info_ref, own_ref, len_ref, table_ref, owner_ref, q_ref, new_k_ref, new_v_ref, k_hbm, v_hbm,
    m_ref, acc_ref, qa_ref, hand_bias_ref, pick_ref,
    k_ref, v_ref, bias_ref, s_ref, mx_ref, sems,
):
    @pl.when(info_ref[3] == 1)
    def _():
        copies = []
        for i in range(4):
            part = pl.ds(i * (TOKENS // 4), TOKENS // 4)
            copies.append(pltpu.make_async_copy(k_hbm.at[part], k_ref.at[part], sems.at[0, i]))
            copies.append(pltpu.make_async_copy(v_hbm.at[part], v_ref.at[part], sems.at[1, i]))
        for copy in copies:
            copy.start()
        me = info_ref[0] * 8 + info_ref[1] * 2 + info_ref[2]
        fill_queries(q_ref, qa_ref)
        sequence = iota((8, 128), 1) // STEPS
        length = jnp.zeros((8, 128), I32)
        start = jnp.zeros((8, 128), I32)
        offset = jnp.int32(0)
        for s in range(SEQS):
            one = len_ref[0, s]
            length = jnp.where(sequence == s, one, length)
            start = jnp.where(sequence == s, offset, start)
            offset = offset + ((one + PAGE_TOKENS - 1) >> 3)
        length, start = length[0:1], start[0:1]
        past = iota((PAGES, 128), 0) - start
        live = jnp.where(past >= 0, jnp.clip(length - past * PAGE_TOKENS, 0, PAGE_TOKENS), 0)
        hot = jnp.where(iota((PAGES, PAGES), 0) == table_ref[...], 1.0, 0.0).astype(BF16)
        of_page = jnp.dot(hot, live.astype(F32).astype(BF16), preferred_element_type=F32)
        page = iota((HAND, PAGES), 0)
        entry = iota((HAND, PAGES), 1)
        named = jnp.where((owner_ref[...] == me) & (entry // (PPD * TOP) == page // 2), 1.0, 0.0)
        total = jnp.sum(named, axis=1, keepdims=True)
        filled = jnp.where(total > (iota((HAND, 1), 0) % 2).astype(F32), 1.0, 0.0)

        def token_bias(tokens, pages):
            wide = jnp.broadcast_to(tokens[:, None, :], (pages, PAGE_TOKENS, 128))
            step = iota((pages, PAGE_TOKENS, 128), 1).astype(F32)
            bias = jnp.where(step < wide, 0.0, -BIG)
            return bias.reshape(pages * PAGE_TOKENS, 128).astype(BF16)

        hand = of_page[:HAND]
        hand_bias_ref[...] = token_bias(hand * filled, HAND)
        bias_ref[0:HAND_TOKENS] = token_bias(hand * (1.0 - filled), HAND)
        bias_ref[HAND_TOKENS:TOKENS] = token_bias(of_page[HAND:], PAGES - HAND)
        new_key, new_row = iota((ROWS, 128), 0), iota((ROWS, 128), 1)
        seen = (new_key // STEPS == new_row // STEPS) & (new_key <= new_row)
        bias_ref[TOKENS : TOKENS + ROWS] = jnp.where(seen, 0.0, -BIG).astype(BF16)
        bias_ref[TOKENS + ROWS :] = jnp.full((CHUNK - ROWS, 128), -BIG, BF16)
        k_ref[TOKENS : TOKENS + ROWS] = new_k_ref[...]
        v_ref[TOKENS : TOKENS + ROWS] = new_v_ref[...]
        k_ref[TOKENS + ROWS :] = jnp.zeros((CHUNK - ROWS, WIDTH), BF16)
        v_ref[TOKENS + ROWS :] = jnp.zeros((CHUNK - ROWS, WIDTH), BF16)
        lane = iota((8, ROWS), 1)
        targets = []
        owners = [own_ref[i] for i in range(PPD * TOP)]
        for t in range(TOP):
            target = jnp.zeros((8, ROWS), I32)
            for p in range(PPD):
                i = p * TOP + t
                rank = jnp.int32(0)
                for e in range(i):
                    rank = rank + jnp.where(owners[e] == owners[i], 1, 0)
                target = jnp.where(lane // PAGE_TOKENS == p, owners[i] * 2 + rank, target)
            targets.append(target[0:1])
        slot = iota((HAND_TOKENS, ROWS), 0)
        column = iota((HAND_TOKENS, ROWS), 1)
        to_slot = (slot // PAGE_TOKENS == targets[0]) | (slot // PAGE_TOKENS == targets[1])
        same = slot % PAGE_TOKENS == column % PAGE_TOKENS
        pick_ref[...] = jnp.where(to_slot & same, 1.0, 0.0).astype(BF16)
        for copy in copies:
            copy.wait()

        def rows(c):
            return pl.ds(pl.multiple_of(c * CHUNK, CHUNK), CHUNK)

        def one_head(j, carry):
            attend(
                j, qa_ref, POOL_CHUNKS,
                lambda c, j: k_ref[rows(c), head_lanes(j)],
                lambda c, j: v_ref[rows(c), head_lanes(j)],
                lambda c: bias_ref[rows(c)],
                s_ref, mx_ref, m_ref, acc_ref, True,
            )
            return carry

        lax.fori_loop(0, KV_HEADS, one_head, 0)


def pool_attend(info, own, lengths, table, owners, q, new_k, new_v, cache_k, cache_v):
    total = POOL_CHUNKS * CHUNK
    smem = pl.BlockSpec(memory_space=pltpu.SMEM)
    hbm = pl.BlockSpec(memory_space=pl.ANY)
    return pl.pallas_call(
        pool_kernel,
        out_shape=STATE
        + [
            jax.ShapeDtypeStruct((KV_HEADS, QROWS, 2 * HEAD_WIDTH), BF16),
            jax.ShapeDtypeStruct((HAND_TOKENS, 128), BF16),
            jax.ShapeDtypeStruct((HAND_TOKENS, ROWS), BF16),
        ],
        in_specs=[smem, smem, smem] + [vmem()] * 5 + [hbm, hbm],
        out_specs=[vmem()] * 5,
        scratch_shapes=[
            pltpu.VMEM((total, WIDTH), BF16),
            pltpu.VMEM((total, WIDTH), BF16),
            pltpu.VMEM((total, 128), BF16),
            pltpu.VMEM((POOL_CHUNKS, QROWS, CHUNK), F32),
            pltpu.VMEM((QROWS, 128), F32),
            pltpu.SemaphoreType.DMA((2, 4)),
        ],
        compiler_params=pltpu.CompilerParams(vmem_limit_bytes=VMEM_LIMIT),
        cost_estimate=pl.CostEstimate(
            flops=4 * KV_HEADS * QROWS * total * 256,
            bytes_accessed=total * WIDTH * 4,
            transcendentals=KV_HEADS * QROWS * total,
        ),
    )(info, own, lengths, table, owners, q, new_k, new_v, cache_k, cache_v)


def pick_kernel(pick_ref, kv_ref, out_ref):
    for i in range(2):
        rows = jnp.dot(pick_ref[...], kv_ref[i], preferred_element_type=F32).astype(BF16)
        out_ref[:, i] = rows.reshape(HAND // 2, 2 * PAGE_TOKENS, WIDTH)


def pick_pages(pick, kv):
    return pl.pallas_call(
        pick_kernel,
        out_shape=jax.ShapeDtypeStruct((HAND // 2, 2, 2 * PAGE_TOKENS, WIDTH), BF16),
        in_specs=[vmem(), vmem()],
        out_specs=vmem(),
        compiler_params=pltpu.CompilerParams(vmem_limit_bytes=VMEM_LIMIT),
    )(pick, kv)


def hand_kernel(arrived_ref, bias_ref, qa_ref, m_in, acc_in, out_ref, s_ref, mx_ref, m_ref, acc_ref):
    m_ref[...] = m_in[...]
    acc_ref[...] = acc_in[...]
    part = CHUNK // (2 * PAGE_TOKENS)

    def chunk(c, i, j):
        at = pl.ds(c * part, part)
        return arrived_ref[at, i, :, head_lanes(j)].reshape(CHUNK, HEAD_WIDTH)

    def one_head(j, carry):
        attend(
            j, qa_ref, HAND_TOKENS // CHUNK,
            lambda c, j: chunk(c, 0, j),
            lambda c, j: chunk(c, 1, j),
            lambda c: bias_ref[pl.ds(pl.multiple_of(c * CHUNK, CHUNK), CHUNK)],
            s_ref, mx_ref, m_ref, acc_ref, False,
        )
        return carry

    lax.fori_loop(0, KV_HEADS, one_head, 0)
    finish(acc_ref, out_ref)


def hand_attend(arrived, bias, qa, m, acc):
    return pl.pallas_call(
        hand_kernel,
        out_shape=jax.ShapeDtypeStruct((ROWS, KV_HEADS * GROUP_WIDTH * HEAD_WIDTH), BF16),
        in_specs=[vmem()] * 5,
        out_specs=vmem(),
        scratch_shapes=[
            pltpu.VMEM((HAND_TOKENS // CHUNK, QROWS, CHUNK), F32),
            pltpu.VMEM((QROWS, 128), F32),
        ]
        + [pltpu.VMEM(s.shape, s.dtype) for s in STATE],
        compiler_params=pltpu.CompilerParams(vmem_limit_bytes=VMEM_LIMIT),
    )(arrived, bias, qa, m, acc)


def body(
    queries, keys, values, page_owner, lengths, page_table, group_cache_keys, group_cache_values
):
    section = lax.axis_index("s")
    x, y, c = place()
    info = jnp.stack([x, y, c, section]).astype(I32)
    me = (x * 4 + y) * 2 + c
    q = queries[0]
    kv = jnp.stack([keys[0], values[0]])

    def first_hop(k):
        def target(x, y, c, s):
            if s == 1:
                return None
            return (x, y + k, c, s) if c == 0 else (x + k, y, c, s)

        return moved(kv, ("x", "y", "c", "s"), target)

    near = [first_hop(k) for k in (1, 2, 3)]
    crossed = moved(kv, ("s",), lambda s: (1,) if s == 0 else None)
    own = lax.dynamic_slice_in_dim(page_owner.reshape(-1), me * PPD * TOP, PPD * TOP)
    m, acc, qa, hand_bias, pick = pool_attend(
        info, own, lengths, page_table, page_owner.reshape(1, PAGES), q, keys[0], values[0],
        group_cache_keys.reshape(TOKENS, WIDTH), group_cache_values.reshape(TOKENS, WIDTH),
    )

    def prompt(q, kv, near, crossed, *_):
        block = jnp.stack([kv] + near)

        def second_hop(k):
            def target(x, y, c):
                return (x + k, y, c) if c == 0 else (x, y + k, c)

            return moved(block, CTX, target)

        def other_core(piece):
            return moved(piece, ("c",), lambda c: (1 - c,))

        block_other = other_core(block)
        far = [second_hop(k) for k in (1, 2, 3)]
        state = prompt_attend(info, q, [block, block_other], [(False, 0), (True, 0)], None, False)
        far_other = [other_core(piece) for piece in far]
        state = prompt_attend(info, q, far, [(False, k) for k in (1, 2, 3)], state, False)
        return prompt_attend(info, q, far_other, [(True, k) for k in (1, 2, 3)], state, True)

    def decode(q, kv, near, crossed, m, acc, qa, hand_bias, pick):
        outgoing = pick_pages(pick, crossed)
        arrived = lax.all_to_all(outgoing, CTX, 0, 0, tiled=True)
        return hand_attend(arrived, hand_bias, qa, m, acc)

    out = lax.cond(
        section == 0, prompt, decode, q, kv, near, crossed, m, acc, qa, hand_bias, pick
    )
    return out[None]


def solution(mesh):
    inner = Mesh(mesh.devices.reshape([SIZES[a] for a in AXES]), AXES)
    return jax.shard_map(
        body,
        mesh=inner,
        in_specs=(
            P("s", CTX, "t"),
            P("s", CTX, "t"),
            P("s", CTX, "t"),
            P(),
            P(CTX, None),
            P(CTX, None),
            P(CTX, None, "t"),
            P(CTX, None, "t"),
        ),
        out_specs=P("s", CTX, "t"),
        check_vma=False,
    )
```

time: 136 us -> 56 us (0.41)
  the two profiles are of different devices: /device:TPU:1 before, /device:TPU:225 now
where the time goes in v1:
time: 56 us; the launch traced here: 55 us
  Pallas kernels  22.8 us (41%)
  blocking collectives  19.2 us (34%)
  local copies, waits for them, and re-layouts  9.43 us (17%)
  starting transfers between devices  3.27 us (6%)
    pallas_call x1, Pallas kernels, pool_attend(): pl.pallas_call(pool_kernel, out_shape=STATE + [jax.ShapeDtypeStruct((KV_H...  20 us
    all_to_all x1, blocking collectives, decode(): arrived = lax.all_to_all(outgoing, CTX, 0, 0, tiled=True)  19.2 us
    unnamed x18, local copies, waits for them, and re-layouts  8.31 us
    ppermute x4, starting transfers between devices, moved(): return lax.ppermute(shard, axes if len(axes) > 1 else axes[0], pairs)  3.27 us
    pallas_call x1, Pallas kernels, hand_attend(): pl.pallas_call(hand_kernel, out_shape=jax.ShapeDtypeStruct((ROWS, KV_HEAD...  2.55 us
  transfers between devices with their start and end apart: 4, of which 0 were waited for; matrix products, arithmetic and copies ran while one was open for 2% of the time, Pallas kernels for 36%

profile of v1, /device:TPU:225, one launch (start us, length us, event | category | flops | bytes accessed | tf_op | source)
XLA Modules:
  0.0 55.0 jit_solution(1339243849112675606)
XLA Ops:
  0.0 0.8 %constant_dynamic-update-slice_fusion.1 = bf16[2,64,256]{2,1,0:T(8,128)(2,1)S(1)} fusion(bf16[1,64,256]{2,1,0:T(8,128)(2,1)} %param.11), kind=kLoop, calls=%fused_computation.2 | loop fusion | bytes 65536
  0.8 0.8 %constant_dynamic-update-slice_fusion = bf16[2,64,256]{2,1,0:T(8,128)(2,1)S(1)} fusion(bf16[2,64,256]{2,1,0:T(8,128)(2,1)S(1)} %constant_dynamic-update-slice_fusion.1, bf16[1,64,256]{2,1,0:T(8,128)(2,1)} %param.12), kind=kLoop, calls=%fused_computation.1 | loop fusion | bytes 65536 | tf_op jit(solution)/shard_map/stack | solution.py:400
  1.5 1.3 %collective-permute-start.7 = (bf16[2,64,256]{2,1,0:T(8,128)(2,1)S(1)}, bf16[2,64,256]{2,1,0:T(8,128)(2,1)S(1)}, u32[]{:S(2)}, u32[]{:S(2)}) collective-permute-start(bf16[2,64,256]{2,1,0:T(8,128)(2,1)S(1)} %constant_dynamic-update-slice_fusion), channel_id=1, source_target_pairs={{0,1},{2,3},{4,5},{6,7},{8,9},{10,11},{12,13},{14,15},{16,17},{18,... | collective-permute-start | bytes 196616 | tf_op jit(solution)/shard_map/ppermute | solution.py:49
  2.8 0.7 %collective-permute-start.10 = (bf16[2,64,256]{2,1,0:T(8,128)(2,1)S(1)}, bf16[2,64,256]{2,1,0:T(8,128)(2,1)S(1)}, u32[]{:S(2)}, u32[]{:S(2)}) collective-permute-start(bf16[2,64,256]{2,1,0:T(8,128)(2,1)S(1)} %constant_dynamic-update-slice_fusion), channel_id=1, source_target_pairs={{0,48},{8,200},{16,0},{24,216},{32,16},{40,232},{48,32},{56,248},{... | collective-permute-start | bytes 196616 | tf_op jit(solution)/shard_map/ppermute | solution.py:49
  3.5 0.7 %collective-permute-start.8 = (bf16[2,64,256]{2,1,0:T(8,128)(2,1)S(1)}, bf16[2,64,256]{2,1,0:T(8,128)(2,1)S(1)}, u32[]{:S(2)}, u32[]{:S(2)}) collective-permute-start(bf16[2,64,256]{2,1,0:T(8,128)(2,1)S(1)} %constant_dynamic-update-slice_fusion), channel_id=1, source_target_pairs={{0,16},{8,72},{16,32},{24,88},{32,48},{40,104},{48,0},{56,120},{64... | collective-permute-start | bytes 196616 | tf_op jit(solution)/shard_map/ppermute | solution.py:49
  4.2 0.7 %collective-permute-start.9 = (bf16[2,64,256]{2,1,0:T(8,128)(2,1)S(1)}, bf16[2,64,256]{2,1,0:T(8,128)(2,1)S(1)}, u32[]{:S(2)}, u32[]{:S(2)}) collective-permute-start(bf16[2,64,256]{2,1,0:T(8,128)(2,1)S(1)} %constant_dynamic-update-slice_fusion), channel_id=1, source_target_pairs={{0,32},{8,136},{16,48},{24,152},{32,0},{40,168},{48,16},{56,184},{... | collective-permute-start | bytes 196616 | tf_op jit(solution)/shard_map/ppermute | solution.py:49
  4.8 0.8 %copy.12 = s32[256,2]{1,0:T(8,128)S(1)} copy(s32[256,2]{0,1:T(2,128)} %param.13) | data formatting | bytes 4096 | tf_op args[3]
  5.6 0.1 reshape.12
  5.8 0.1 reshape.13.owner_ref
  6.0 0.1 dynamic_slice.3.own_ref
  6.0 0.1 pad_add_fusion.info_ref
  6.1 0.0 copy-start
  6.1 0.8 %copy-done = bf16[1,64,256]{2,1,0:T(8,128)(2,1)S(1)} copy-done((bf16[1,64,256]{2,1,0:T(8,128)(2,1)S(1)}, bf16[1,64,256]{2,1,0:T(8,128)(2,1)}, u32[]{:S(2)}) %copy-start) | copy-done | bytes 32792
  6.9 0.0 copy-start.1
  6.9 0.8 %copy-done.1 = bf16[1,64,256]{2,1,0:T(8,128)(2,1)S(1)} copy-done((bf16[1,64,256]{2,1,0:T(8,128)(2,1)S(1)}, bf16[1,64,256]{2,1,0:T(8,128)(2,1)}, u32[]{:S(2)}) %copy-start.1) | copy-done | bytes 32792
  7.6 0.0 copy-start.2
  7.6 1.6 %copy-done.2 = bf16[512,8,256]{2,1,0:T(8,128)(2,1)S(1)} copy-done((bf16[512,8,256]{2,1,0:T(8,128)(2,1)S(1)}, bf16[512,8,256]{2,1,0:T(8,128)(2,1)}, u32[]{:S(2)}) %copy-start.2) | copy-done | bytes 2097176
  9.2 0.0 copy-start.3
  9.2 1.6 %copy-done.3 = bf16[512,8,256]{2,1,0:T(8,128)(2,1)S(1)} copy-done((bf16[512,8,256]{2,1,0:T(8,128)(2,1)S(1)}, bf16[512,8,256]{2,1,0:T(8,128)(2,1)}, u32[]{:S(2)}) %copy-start.3) | copy-done | bytes 2097176
  10.8 0.0 copy-start.4
  10.8 0.7 %copy-done.4 = s32[1,512]{1,0:T(1,128)S(1)} copy-done((s32[1,512]{1,0:T(1,128)S(1)}, s32[1,512]{1,0:T(1,128)}, u32[]{:S(2)}) %copy-start.4) | copy-done | bytes 2072
  11.5 0.0 copy-start.5
  11.5 0.7 %copy-done.5 = s32[1,16]{1,0:T(1,128)S(1)} copy-done((s32[1,16]{1,0:T(1,128)S(1)}, s32[1,16]{1,0:T(1,128)}, u32[]{:S(2)}) %copy-start.5) | copy-done | bytes 88
  12.1 0.0 copy-start.7
  12.1 20.0 %shard_map.84 = (f32[2,512,128]{2,1,0:T(8,128)S(1)}, f32[2,512,256]{2,1,0:T(8,128)S(1)}, bf16[2,512,256]{2,1,0:T(8,128)(2,1)S(1)}, bf16[512,128]{1,0:T(8,128)(2,1)S(1)}, bf16[512,64]{1,0:T(8,128)(2,1)S(1)}) custom-call(s32[4]{0:T(128)S(1)} %pad_add_fusion.info_ref, s32[16]{0:T(128)S(1)} %dynamic_slice.3.own_ref, s32[1,16]{1,0:T(1,128)S(1)} %copy-done.5, ...), custom_call_target="tpu_custom_call" | custom-call | flops 4563402752 | bytes 4456448 | tf_op jit(solution)/shard_map/pallas_call | solution.py:311
  32.2 0.0 collective-permute-done.10
  32.2 0.0 collective-permute-done.8
  32.2 0.0 collective-permute-done.9
  32.2 0.0 collective-permute-done.7
  32.2 0.0 copy-done.7
  32.2 22.0 %conditional.1 = (bf16[1,64,2048]{2,1,0:T(8,128)(2,1)S(1)}) conditional(s32[]{:T(128)} %convert_element_type.3, (bf16[512,64]{1,0:T(8,128)(2,1)S(1)}, bf16[2,64,256]{2,1,0:T(8,128)(2,1)S(1)}, bf16[512,128]{1,0:T(8,128)(2,1)S(1)}, bf16[2,512,256]{2,1,0:T(8,128)(2,1)S(1)}, f32[2,512,128]{2,1,0:T(8,128)S(1)}, ...), branch_computations={%region_0.0_spmd, %region_1.0_spmd} | conditional | flops 2147876864 | bytes 9961760 | solution.py:442
  32.3 0.3 branch_0_fun.2
  32.5 19.2 %all_to_all.4.arrived_ref = bf16[32,2,16,256]{3,2,1,0:T(8,128)(2,1)S(1)} all-to-all(bf16[32,2,16,256]{3,2,1,0:T(8,128)(2,1)S(1)} %branch_0_fun.2), channel_id=1, replica_groups=mesh['x'=4,'y'=4,'c'=2,'t'=4,'s'=2] {'x','y','c'}, dimensions={0} | all-to-all | bytes 1048576 | tf_op jit(solution)/shard_map/cond/branch_0_fun/all_to_all | solution.py:439
  51.7 2.5 %branch_0_fun.3 = bf16[64,2048]{1,0:T(8,128)(2,1)S(1)} custom-call(bf16[32,2,16,256]{3,2,1,0:T(8,128)(2,1)S(1)} %all_to_all.4.arrived_ref, bf16[512,128]{1,0:T(8,128)(2,1)S(1)} %get-tuple-element.35.bias_ref, bf16[2,512,256]{2,1,0:T(8,128)(2,1)S(1)} %get-tuple-element.36.qa_ref, f32[2,512,128]{2,1,0:T(8,128)S(1)} %get-tuple-element.37.m_in, ...), custom_call_target="tpu_custom_call" | custom-call | tf_op jit(solution)/shard_map/cond/branch_0_fun/pallas_call | solution.py:378
  54.3 0.0 copy-start.6
  54.3 0.7 %copy-done.6 = bf16[1,64,2048]{2,1,0:T(8,128)(2,1)} copy-done((bf16[1,64,2048]{2,1,0:T(8,128)(2,1)}, bf16[1,64,2048]{2,1,0:T(8,128)(2,1)S(1)}, u32[]{:S(2)}) %copy-start.6) | copy-done | bytes 262168
Async XLA Ops:
  1.5 30.7 %collective-permute-start.7 = (bf16[2,64,256]{2,1,0:T(8,128)(2,1)S(1)}, bf16[2,64,256]{2,1,0:T(8,128)(2,1)S(1)}, u32[]{:S(2)}, u32[]{:S(2)}) collective-permute-start(bf16[2,64,256]{2,1,0:T(8,128)(2,1)S(1)} %constant_dynamic-update-slice_fusion), channel_id=1, source_target_pairs={{0,1},{2,3},{4,5},{6,7},{8,9},{10,11},{12,13},{14,15},{16,17},{18,... | collective-permute-start | bytes 196616 | tf_op jit(solution)/shard_map/ppermute | solution.py:49
  2.8 29.4 %collective-permute-start.10 = (bf16[2,64,256]{2,1,0:T(8,128)(2,1)S(1)}, bf16[2,64,256]{2,1,0:T(8,128)(2,1)S(1)}, u32[]{:S(2)}, u32[]{:S(2)}) collective-permute-start(bf16[2,64,256]{2,1,0:T(8,128)(2,1)S(1)} %constant_dynamic-update-slice_fusion), channel_id=1, source_target_pairs={{0,48},{8,200},{16,0},{24,216},{32,16},{40,232},{48,32},{56,248},{... | collective-permute-start | bytes 196616 | tf_op jit(solution)/shard_map/ppermute | solution.py:49
  3.5 28.7 %collective-permute-start.8 = (bf16[2,64,256]{2,1,0:T(8,128)(2,1)S(1)}, bf16[2,64,256]{2,1,0:T(8,128)(2,1)S(1)}, u32[]{:S(2)}, u32[]{:S(2)}) collective-permute-start(bf16[2,64,256]{2,1,0:T(8,128)(2,1)S(1)} %constant_dynamic-update-slice_fusion), channel_id=1, source_target_pairs={{0,16},{8,72},{16,32},{24,88},{32,48},{40,104},{48,0},{56,120},{64... | collective-permute-start | bytes 196616 | tf_op jit(solution)/shard_map/ppermute | solution.py:49
  4.2 28.1 %collective-permute-start.9 = (bf16[2,64,256]{2,1,0:T(8,128)(2,1)S(1)}, bf16[2,64,256]{2,1,0:T(8,128)(2,1)S(1)}, u32[]{:S(2)}, u32[]{:S(2)}) collective-permute-start(bf16[2,64,256]{2,1,0:T(8,128)(2,1)S(1)} %constant_dynamic-update-slice_fusion), channel_id=1, source_target_pairs={{0,32},{8,136},{16,48},{24,152},{32,0},{40,168},{48,16},{56,184},{... | collective-permute-start | bytes 196616 | tf_op jit(solution)/shard_map/ppermute | solution.py:49
  6.1 0.8 %copy-start = (bf16[1,64,256]{2,1,0:T(8,128)(2,1)S(1)}, bf16[1,64,256]{2,1,0:T(8,128)(2,1)}, u32[]{:S(2)}) copy-start(bf16[1,64,256]{2,1,0:T(8,128)(2,1)} %param.11) | copy-start | bytes 98308
  6.9 0.8 %copy-start.1 = (bf16[1,64,256]{2,1,0:T(8,128)(2,1)S(1)}, bf16[1,64,256]{2,1,0:T(8,128)(2,1)}, u32[]{:S(2)}) copy-start(bf16[1,64,256]{2,1,0:T(8,128)(2,1)} %param.12) | copy-start | bytes 98308
  7.6 1.6 %copy-start.2 = (bf16[512,8,256]{2,1,0:T(8,128)(2,1)S(1)}, bf16[512,8,256]{2,1,0:T(8,128)(2,1)}, u32[]{:S(2)}) copy-start(bf16[512,8,256]{2,1,0:T(8,128)(2,1)} %param.16) | copy-start | bytes 6291460
  9.2 1.6 %copy-start.3 = (bf16[512,8,256]{2,1,0:T(8,128)(2,1)S(1)}, bf16[512,8,256]{2,1,0:T(8,128)(2,1)}, u32[]{:S(2)}) copy-start(bf16[512,8,256]{2,1,0:T(8,128)(2,1)} %param.17) | copy-start | bytes 6291460
  10.8 0.7 %copy-start.4 = (s32[1,512]{1,0:T(1,128)S(1)}, s32[1,512]{1,0:T(1,128)}, u32[]{:S(2)}) copy-start(s32[1,512]{1,0:T(1,128)} %table_ref.1) | copy-start | bytes 6148
  11.5 0.7 %copy-start.5 = (s32[1,16]{1,0:T(1,128)S(1)}, s32[1,16]{1,0:T(1,128)}, u32[]{:S(2)}) copy-start(s32[1,16]{1,0:T(1,128)} %len_ref.1) | copy-start | bytes 196
  12.1 20.1 %copy-start.7 = (bf16[1,64,2048]{2,1,0:T(8,128)(2,1)S(1)}, bf16[1,64,2048]{2,1,0:T(8,128)(2,1)}, u32[]{:S(2)}) copy-start(bf16[1,64,2048]{2,1,0:T(8,128)(2,1)} %param.10) | copy-start | bytes 786436
  54.3 0.7 %copy-start.6 = (bf16[1,64,2048]{2,1,0:T(8,128)(2,1)}, bf16[1,64,2048]{2,1,0:T(8,128)(2,1)S(1)}, u32[]{:S(2)}) copy-start(bf16[1,64,2048]{2,1,0:T(8,128)(2,1)S(1)} %get-tuple-element.76) | copy-start | bytes 786436

commit v2 on v1

v2 whole, which is shorter than its diff:
```python
import math

import jax
import jax.numpy as jnp
import numpy as np
from jax import lax
from jax.experimental import pallas as pl
from jax.experimental.pallas import tpu as pltpu
from jax.sharding import Mesh
from jax.sharding import PartitionSpec as P

HEAD_WIDTH = 128
GROUP_WIDTH = 8
KV_HEADS = 2
ROWS = 64
QROWS = GROUP_WIDTH * ROWS
WIDTH = KV_HEADS * HEAD_WIDTH
QUERY_WIDTH = GROUP_WIDTH * WIDTH
PAGE_TOKENS = 8
PAGES = 512
HAND = 64
SEQS = 16
STEPS = 4
TOP = 2
PPD = 8
PROMPT_PAGES = 256
TOKENS = PAGES * PAGE_TOKENS
HAND_TOKENS = HAND * PAGE_TOKENS
CHUNK = 512
NEW = 128
BIG = float(2**20)
TO_LOG2 = HEAD_WIDTH**-0.5 * math.log2(math.e)
SIDE = 4
AXES = ("x", "y", "c", "t", "s")
SIZES = {"x": 4, "y": 4, "c": 2, "t": 4, "s": 2}
CTX = ("x", "y", "c")
VMEM_LIMIT = 40 * 1024 * 1024
F32 = jnp.float32
BF16 = jnp.bfloat16
I32 = jnp.int32
HBM = pl.BlockSpec(memory_space=pltpu.HBM)
VMEM = pl.BlockSpec(memory_space=pltpu.VMEM)
STATE = [
    jax.ShapeDtypeStruct((KV_HEADS, QROWS, 128), F32),
    jax.ShapeDtypeStruct((KV_HEADS, QROWS, 2 * HEAD_WIDTH), F32),
]
ASKED = jax.ShapeDtypeStruct((KV_HEADS, QROWS, 2 * HEAD_WIDTH), BF16)
ANSWER = jax.ShapeDtypeStruct((ROWS, QUERY_WIDTH), BF16)


def moved(shard, axes, target):
    sizes = [SIZES[a] for a in axes]
    pairs = []
    for source in range(math.prod(sizes)):
        place = [int(i) for i in np.unravel_index(source, sizes)]
        goal = target(*place)
        if goal is not None:
            goal = [a % b for a, b in zip(goal, sizes)]
            pairs.append((source, int(np.ravel_multi_index(goal, sizes))))
    return lax.ppermute(shard, axes if len(axes) > 1 else axes[0], pairs)


def cost(keys):
    return pl.CostEstimate(
        flops=4 * KV_HEADS * QROWS * keys * 256,
        bytes_accessed=keys * WIDTH * 4,
        transcendentals=KV_HEADS * QROWS * keys,
    )


def iota(shape, axis):
    return lax.broadcasted_iota(I32, shape, axis)


def lanes(j):
    return pl.ds(pl.multiple_of(j * HEAD_WIDTH, HEAD_WIDTH), HEAD_WIDTH)


def ask(q_hbm, qa_ref, sem):
    copies = []
    for h in range(KV_HEADS * GROUP_WIDTH):
        source = q_hbm.at[:, pl.ds(h * HEAD_WIDTH, HEAD_WIDTH)]
        j, g = divmod(h, GROUP_WIDTH)
        goal = qa_ref.at[j, pl.ds(g * ROWS, ROWS), pl.ds(0, HEAD_WIDTH)]
        copies.append(pltpu.make_async_copy(source, goal, sem.at[h]))
    return copies


def mark_rows(qa_ref):
    hot = jnp.where(iota((QROWS, 128), 0) % ROWS == iota((QROWS, 128), 1), 1.0, 0.0).astype(BF16)
    for j in range(KV_HEADS):
        qa_ref[j, :, HEAD_WIDTH:] = hot


def score(q, keys, bias):
    wide = jnp.concatenate([keys, bias], axis=1)
    return lax.dot_general(q, wide, (((1,), (1,)), ((), ())), preferred_element_type=F32)


def peak(s):
    parts = [s[:, i : i + 128] for i in range(0, s.shape[1], 128)]
    while len(parts) > 1:
        pairs = [jnp.maximum(a, b) for a, b in zip(parts[::2], parts[1::2])]
        parts = pairs + parts[len(parts) // 2 * 2 :]
    return parts[0]


def spread(column):
    return jnp.broadcast_to(jnp.max(column, axis=1, keepdims=True), (QROWS, 128))


def mix(s, low, values):
    lows = jnp.concatenate([low] * (s.shape[1] // 128), axis=1)
    weights = jnp.exp2(s * TO_LOG2 - lows).astype(BF16)
    wide = jnp.concatenate([values, jnp.ones((values.shape[0], HEAD_WIDTH), BF16)], axis=1)
    return jnp.dot(weights, wide, preferred_element_type=F32)


def attend(j, qa_ref, keys, values, bias, s_ref, m_in, acc_in):
    s = score(qa_ref[j], keys, bias)
    s_ref[j] = s
    column = peak(s)
    if m_in is not None:
        column = jnp.maximum(column, m_in[j])
    top = spread(column)
    low = top * TO_LOG2
    total = mix(s_ref[j], low, values)
    if m_in is not None:
        shrink = jnp.exp2(m_in[j] * TO_LOG2 - low)
        total = total + acc_in[j] * jnp.concatenate([shrink, shrink], axis=1)
    return top, total


def answer(j, total, answer_ref, out_hbm, sems):
    result = (total[:, :HEAD_WIDTH] / total[:, HEAD_WIDTH:]).astype(BF16)
    for g in range(GROUP_WIDTH):
        at = (j * GROUP_WIDTH + g) * HEAD_WIDTH
        answer_ref[:, at : at + HEAD_WIDTH] = result[g * ROWS : (g + 1) * ROWS]
    part = pl.ds(j * GROUP_WIDTH * HEAD_WIDTH, GROUP_WIDTH * HEAD_WIDTH)
    copy = pltpu.make_async_copy(answer_ref.at[:, part], out_hbm.at[:, part], sems.at[j])
    copy.start()
    return copy


ANSWER_SCRATCH = [pltpu.VMEM(ANSWER.shape, BF16), pltpu.SemaphoreType.DMA((KV_HEADS,))]


def prompt_kernel(pieces, first, last, *refs):
    count = len(pieces)
    keys_in_all = count * SIDE * ROWS
    if first:
        q_hbm, *refs = refs
    else:
        qa_ref, m_in, acc_in, *refs = refs
    piece_refs, refs = refs[:count], refs[count:]
    if last:
        out_hbm, *refs = refs
    else:
        m_ref, acc_ref, *refs = refs
    if first:
        qa_ref, *refs = refs
    bias_ref, s_ref, *refs = refs
    if first:
        copies = ask(q_hbm, qa_ref, refs[0])
        for copy in copies:
            copy.start()
        mark_rows(qa_ref)
    x, y, c = lax.axis_index("x"), lax.axis_index("y"), lax.axis_index("c")
    me = x * 8 + y * 2 + c
    row_pos = me * ROWS + iota((ROWS, 128), 1)
    for i, (swapped, k2) in enumerate(pieces):
        core = (1 - c) if swapped else c
        for k1 in range(SIDE):
            on_x = jnp.where(core == 0, k2, k1)
            on_y = jnp.where(core == 0, k1, k2)
            block = ((x - on_x) & 3) * 8 + ((y - on_y) & 3) * 2 + core
            key_pos = block * ROWS + iota((ROWS, 128), 0)
            bias = jnp.where(key_pos > row_pos, -BIG, 0.0).astype(BF16)
            at = (i * SIDE + k1) * ROWS
            bias_ref[at : at + ROWS, :] = bias
    if first:
        for copy in copies:
            copy.wait()

    def piece_rows(half, j):
        head = slice(j * HEAD_WIDTH, (j + 1) * HEAD_WIDTH)
        rows = slice(half * ROWS, (half + 1) * ROWS)
        parts = [ref[:, rows, head].reshape(SIDE * ROWS, HEAD_WIDTH) for ref in piece_refs]
        return jnp.concatenate(parts, axis=0)

    sent = []
    for j in range(KV_HEADS):
        top, total = attend(
            j, qa_ref, piece_rows(0, j), piece_rows(1, j), bias_ref[...], s_ref,
            None if first else m_in, None if first else acc_in,
        )
        if last:
            sent.append(answer(j, total, refs[0], out_hbm, refs[1]))
        else:
            m_ref[j] = top
            acc_ref[j] = total
    for copy in sent:
        copy.wait()


def prompt_attend(arrays, pieces, q=None, state=None, last=False):
    first = state is None
    keys = len(pieces) * SIDE * ROWS
    scratch = [pltpu.VMEM((keys, 128), BF16), pltpu.VMEM((KV_HEADS, QROWS, keys), F32)]
    if first:
        scratch.append(pltpu.SemaphoreType.DMA((KV_HEADS * GROUP_WIDTH,)))
    if last:
        scratch += ANSWER_SCRATCH

    def kernel(*refs):
        prompt_kernel(pieces, first, last, *refs)

    before = [q] if first else list(state)
    return pl.pallas_call(
        kernel,
        out_shape=ANSWER if last else STATE + [ASKED] * first,
        in_specs=([HBM] if first else [VMEM] * 3) + [VMEM] * len(pieces),
        out_specs=HBM if last else [VMEM] * (2 + first),
        scratch_shapes=scratch,
        compiler_params=pltpu.CompilerParams(vmem_limit_bytes=VMEM_LIMIT),
        cost_estimate=cost(keys),
    )(*before, *arrays)


def pool_kernel(
    len_hbm, table_hbm, owner_hbm, q_hbm, new_k_hbm, new_v_hbm, k_hbm, v_hbm,
    m_ref, acc_ref, qa_ref, hand_bias_ref, pick_ref,
    k_ref, v_ref, new_k_ref, new_v_ref, bias_ref, new_bias_ref, s_ref, new_s_ref, mx_ref,
    len_ref, table_ref, owner_ref, own_ref, sems, ask_sems,
):
    @pl.when(lax.axis_index("s") == 1)
    def _():
        small = [
            pltpu.make_async_copy(len_hbm, len_ref, sems.at[0]),
            pltpu.make_async_copy(table_hbm, table_ref, sems.at[1]),
            pltpu.make_async_copy(owner_hbm, owner_ref, sems.at[2]),
            pltpu.make_async_copy(owner_hbm, own_ref, sems.at[3]),
        ]
        large = ask(q_hbm, qa_ref, ask_sems) + [
            pltpu.make_async_copy(new_k_hbm, new_k_ref.at[pl.ds(0, ROWS)], sems.at[4]),
            pltpu.make_async_copy(new_v_hbm, new_v_ref.at[pl.ds(0, ROWS)], sems.at[5]),
            pltpu.make_async_copy(k_hbm, k_ref, sems.at[6]),
            pltpu.make_async_copy(v_hbm, v_ref, sems.at[7]),
        ]
        for copy in small + large:
            copy.start()
        me = lax.axis_index("x") * 8 + lax.axis_index("y") * 2 + lax.axis_index("c")
        mark_rows(qa_ref)
        new_key, new_row = iota((NEW, 128), 0), iota((NEW, 128), 1)
        seen = (new_key // STEPS == new_row // STEPS) & (new_key <= new_row)
        new_bias_ref[...] = jnp.where(seen & (new_key < ROWS), 0.0, -BIG).astype(BF16)
        new_k_ref[ROWS:] = jnp.zeros((NEW - ROWS, WIDTH), BF16)
        new_v_ref[ROWS:] = jnp.zeros((NEW - ROWS, WIDTH), BF16)
        for copy in small:
            copy.wait()
        sequence = iota((8, 128), 1) // STEPS
        length = jnp.zeros((8, 128), I32)
        start = jnp.zeros((8, 128), I32)
        offset = jnp.int32(0)
        for s in range(SEQS):
            one = len_ref[0, s]
            length = jnp.where(sequence == s, one, length)
            start = jnp.where(sequence == s, offset, start)
            offset = offset + ((one + PAGE_TOKENS - 1) >> 3)
        length, start = length[0:1], start[0:1]
        past = iota((PAGES, 128), 0) - start
        live = jnp.where(past >= 0, jnp.clip(length - past * PAGE_TOKENS, 0, PAGE_TOKENS), 0)
        hot = jnp.where(iota((PAGES, PAGES), 0) == table_ref[...], 1.0, 0.0).astype(BF16)
        of_page = jnp.dot(hot, live.astype(F32).astype(BF16), preferred_element_type=F32)
        page = iota((HAND, PROMPT_PAGES), 0)
        same_index = iota((HAND, PROMPT_PAGES), 1) // PPD == page // 2
        named = jnp.zeros((HAND, PROMPT_PAGES), F32)
        for t in range(TOP):
            named = named + jnp.where((owner_ref[t : t + 1] == me) & same_index, 1.0, 0.0)
        total = jnp.sum(named, axis=1, keepdims=True)
        filled = jnp.where(total > (iota((HAND, 1), 0) % 2).astype(F32), 1.0, 0.0)

        def token_bias(tokens, pages):
            wide = jnp.broadcast_to(tokens[:, None, :], (pages, PAGE_TOKENS, 128))
            step = iota((pages, PAGE_TOKENS, 128), 1).astype(F32)
            bias = jnp.where(step < wide, 0.0, -BIG)
            return bias.reshape(pages * PAGE_TOKENS, 128).astype(BF16)

        hand = of_page[:HAND]
        hand_bias_ref[...] = token_bias(hand * filled, HAND)
        bias_ref[0:HAND_TOKENS] = token_bias(hand * (1.0 - filled), HAND)
        bias_ref[HAND_TOKENS:TOKENS] = token_bias(of_page[HAND:], PAGES - HAND)
        lane = iota((8, ROWS), 1)
        owners = [own_ref[i % TOP, me * PPD + i // TOP] for i in range(PPD * TOP)]
        targets = []
        for t in range(TOP):
            target = jnp.zeros((8, ROWS), I32)
            for p in range(PPD):
                i = p * TOP + t
                rank = jnp.int32(0)
                for e in range(i):
                    rank = rank + jnp.where(owners[e] == owners[i], 1, 0)
                target = jnp.where(lane // PAGE_TOKENS == p, owners[i] * 2 + rank, target)
            targets.append(target[0:1])
        slot = iota((HAND_TOKENS, ROWS), 0)
        column = iota((HAND_TOKENS, ROWS), 1)
        to_slot = (slot // PAGE_TOKENS == targets[0]) | (slot // PAGE_TOKENS == targets[1])
        same = slot % PAGE_TOKENS == column % PAGE_TOKENS
        pick_ref[...] = jnp.where(to_slot & same, 1.0, 0.0).astype(BF16)
        for copy in large:
            copy.wait()

        def rows(c):
            return pl.ds(pl.multiple_of(c * CHUNK, CHUNK), CHUNK)

        def one_head(j, carry):
            s = score(qa_ref[j], new_k_ref[:, lanes(j)], new_bias_ref[...])
            new_s_ref[...] = s
            mx_ref[...] = s

            def scores(c, carry):
                s = score(qa_ref[j], k_ref[rows(c), lanes(j)], bias_ref[rows(c)])
                s_ref[c] = s
                mx_ref[...] = jnp.maximum(mx_ref[...], peak(s))
                return carry

            lax.fori_loop(0, TOKENS // CHUNK, scores, 0, unroll=4)
            top = spread(mx_ref[...])
            m_ref[j] = top
            mx_ref[...] = top * TO_LOG2
            acc_ref[j] = mix(new_s_ref[...], mx_ref[...], new_v_ref[:, lanes(j)])

            def mixes(c, carry):
                acc_ref[j] += mix(s_ref[c], mx_ref[...], v_ref[rows(c), lanes(j)])
                return carry

            lax.fori_loop(0, TOKENS // CHUNK, mixes, 0, unroll=4)
            return carry

        lax.fori_loop(0, KV_HEADS, one_head, 0)


def pool_attend(lengths, table, owners, q, new_k, new_v, cache_k, cache_v):
    return pl.pallas_call(
        pool_kernel,
        out_shape=STATE
        + [
            ASKED,
            jax.ShapeDtypeStruct((HAND_TOKENS, 128), BF16),
            jax.ShapeDtypeStruct((HAND_TOKENS, ROWS), BF16),
        ],
        in_specs=[HBM] * 8,
        out_specs=[VMEM] * 5,
        scratch_shapes=[
            pltpu.VMEM((TOKENS, WIDTH), BF16),
            pltpu.VMEM((TOKENS, WIDTH), BF16),
            pltpu.VMEM((NEW, WIDTH), BF16),
            pltpu.VMEM((NEW, WIDTH), BF16),
            pltpu.VMEM((TOKENS, 128), BF16),
            pltpu.VMEM((NEW, 128), BF16),
            pltpu.VMEM((TOKENS // CHUNK, QROWS, CHUNK), F32),
            pltpu.VMEM((QROWS, NEW), F32),
            pltpu.VMEM((QROWS, 128), F32),
            pltpu.SMEM((1, SEQS), I32),
            pltpu.VMEM((1, PAGES), I32),
            pltpu.VMEM((TOP, PROMPT_PAGES), I32),
            pltpu.SMEM((TOP, PROMPT_PAGES), I32),
            pltpu.SemaphoreType.DMA((8,)),
            pltpu.SemaphoreType.DMA((KV_HEADS * GROUP_WIDTH,)),
        ],
        compiler_params=pltpu.CompilerParams(vmem_limit_bytes=VMEM_LIMIT),
        cost_estimate=cost(TOKENS + NEW),
    )(lengths, table, owners, q, new_k, new_v, cache_k, cache_v)


def pick_kernel(pick_ref, kv_ref, out_ref):
    for i in range(2):
        part = kv_ref[i * ROWS : (i + 1) * ROWS]
        rows = jnp.dot(pick_ref[...], part, preferred_element_type=F32).astype(BF16)
        out_ref[:, i] = rows.reshape(HAND // 2, 2 * PAGE_TOKENS, WIDTH)


def pick_pages(pick, kv):
    return pl.pallas_call(
        pick_kernel,
        out_shape=jax.ShapeDtypeStruct((HAND // 2, 2, 2 * PAGE_TOKENS, WIDTH), BF16),
        in_specs=[VMEM, VMEM],
        out_specs=VMEM,
        compiler_params=pltpu.CompilerParams(vmem_limit_bytes=VMEM_LIMIT),
    )(pick, kv)


def hand_kernel(arrived_ref, bias_ref, qa_ref, m_in, acc_in, out_hbm, s_ref, answer_ref, sems):
    sent = []
    for j in range(KV_HEADS):
        head = slice(j * HEAD_WIDTH, (j + 1) * HEAD_WIDTH)
        _, total = attend(
            j, qa_ref,
            arrived_ref[:, 0, :, head].reshape(HAND_TOKENS, HEAD_WIDTH),
            arrived_ref[:, 1, :, head].reshape(HAND_TOKENS, HEAD_WIDTH),
            bias_ref[...], s_ref, m_in, acc_in,
        )
        sent.append(answer(j, total, answer_ref, out_hbm, sems))
    for copy in sent:
        copy.wait()


def hand_attend(arrived, bias, qa, m, acc):
    return pl.pallas_call(
        hand_kernel,
        out_shape=ANSWER,
        in_specs=[VMEM] * 5,
        out_specs=HBM,
        scratch_shapes=[pltpu.VMEM((KV_HEADS, QROWS, HAND_TOKENS), F32)] + ANSWER_SCRATCH,
        compiler_params=pltpu.CompilerParams(vmem_limit_bytes=VMEM_LIMIT),
        cost_estimate=cost(HAND_TOKENS),
    )(arrived, bias, qa, m, acc)


def body(
    queries, keys, values, page_owner, lengths, page_table, group_cache_keys, group_cache_values
):
    section = lax.axis_index("s")
    q = queries[0]
    kv = jnp.concatenate([keys[0], values[0]], axis=0)

    def first_hop(k):
        def target(x, y, c, s):
            if s == 1:
                return None
            return (x, y + k, c, s) if c == 0 else (x + k, y, c, s)

        return moved(kv, ("x", "y", "c", "s"), target)

    near = [first_hop(k) for k in (1, 3, 2)]
    later_kv, near[0] = lax.optimization_barrier((kv, near[0]))
    crossed = moved(later_kv, ("s",), lambda s: (1,) if s == 0 else None)
    m, acc, qa, hand_bias, pick = pool_attend(
        lengths, page_table, page_owner.T, q, keys[0], values[0],
        group_cache_keys.reshape(TOKENS, WIDTH), group_cache_values.reshape(TOKENS, WIDTH),
    )

    def prompt(q, kv, near, crossed, *_):
        block = jnp.stack([kv, near[0], near[2], near[1]])

        def second_hop(k):
            def target(x, y, c):
                return (x + k, y, c) if c == 0 else (x, y + k, c)

            return moved(block, CTX, target)

        def other_core(piece):
            return moved(piece, ("c",), lambda c: (1 - c,))

        block_other = other_core(block)
        hops = (1, 3, 2)
        far = [second_hop(k) for k in hops]
        m, acc, qa = prompt_attend([block, block_other], [(False, 0), (True, 0)], q=q)
        far, m, acc, qa = lax.optimization_barrier((far, m, acc, qa))
        far_other = [other_core(piece) for piece in far]
        m, acc = prompt_attend(far, [(False, k) for k in hops], state=(qa, m, acc))
        return prompt_attend(
            far_other, [(True, k) for k in hops], state=(qa, m, acc), last=True
        )

    def decode(q, kv, near, crossed, m, acc, qa, hand_bias, pick):
        outgoing = pick_pages(pick, crossed)
        arrived = lax.all_to_all(outgoing, CTX, 0, 0, tiled=True)
        return hand_attend(arrived, hand_bias, qa, m, acc)

    out = lax.cond(
        section == 0, prompt, decode, q, kv, near, crossed, m, acc, qa, hand_bias, pick
    )
    return out[None]


def solution(mesh):
    inner = Mesh(mesh.devices.reshape([SIZES[a] for a in AXES]), AXES)
    return jax.shard_map(
        body,
        mesh=inner,
        in_specs=(
            P("s", CTX, "t"),
            P("s", CTX, "t"),
            P("s", CTX, "t"),
            P(),
            P(CTX, None),
            P(CTX, None),
            P(CTX, None, "t"),
            P(CTX, None, "t"),
        ),
        out_specs=P("s", CTX, "t"),
        check_vma=False,
    )
```

time: 56 us -> 42 us (0.75)
  Pallas kernels: 22.8 us -> 10.5 us
  local copies, waits for them, and re-layouts: 9.43 us -> 7.41 us
  other arithmetic: 0.08 us -> 0.78 us
    pallas_call x2, Pallas kernels: 22.6 us -> 10.2 us  [the longest x1 8.47 us: pool_attend(): pl.pallas_call(pool_kernel, out_shape=STATE + [ASKED, jax.ShapeDtypeStruc...]
    unnamed x18, local copies, waits for them, and re-layouts: 8.31 us -> 7.41 us
    concatenate x0 -> x1, other arithmetic: none -> 0.78 us  [body(): kv = jnp.concatenate([keys[0], values[0]], axis=0)]
    another operation x1 -> x0, local copies, waits for them, and re-layouts: 0.76 us -> none  [body(): kv = jnp.stack([keys[0], values[0]])]
  transfers between devices with their start and end apart: 4 -> 4, of which waited for: 0 -> 0; matrix products, arithmetic and copies ran while one was open for 2% -> 0% of each run, Pallas kernels for 36% -> 20%
where the time goes in v2:
time: 42 us; the launch traced here: 41.5 us
  blocking collectives  19.2 us (46%)
  Pallas kernels  10.5 us (25%)
  local copies, waits for them, and re-layouts  7.41 us (18%)
  starting transfers between devices  3.27 us (8%)
  other arithmetic  0.78 us (2%)
    all_to_all x1, blocking collectives, decode(): arrived = lax.all_to_all(outgoing, CTX, 0, 0, tiled=True)  19.2 us
    pallas_call x1, Pallas kernels, pool_attend(): pl.pallas_call(pool_kernel, out_shape=STATE + [ASKED, jax.ShapeDtypeStruc...  8.47 us
    unnamed x18, local copies, waits for them, and re-layouts  7.41 us
    ppermute x4, starting transfers between devices, moved(): return lax.ppermute(shard, axes if len(axes) > 1 else axes[0], pairs)  3.27 us
    pallas_call x1, Pallas kernels, hand_attend(): pl.pallas_call(hand_kernel, out_shape=ANSWER, in_specs=[VMEM] * 5, out_sp...  1.72 us
  transfers between devices with their start and end apart: 4, of which 0 were waited for; matrix products, arithmetic and copies ran while one was open for 0% of the time, Pallas kernels for 20%

profile of v2, /device:TPU:225, one launch (start us, length us, event | category | flops | bytes accessed | tf_op | source)
XLA Modules:
  0.0 41.5 jit_solution(8397717323304153915)
XLA Ops:
  0.0 0.8 %pad_maximum_fusion.1 = bf16[128,256]{1,0:T(8,128)(2,1)S(1)} fusion(bf16[64,256]{1,0:T(8,128)(2,1)} %bitcast.14, bf16[64,256]{1,0:T(8,128)(2,1)} %bitcast.12), kind=kLoop, calls=%fused_computation.1 | loop fusion | flops 131072 | bytes 131072 | tf_op jit(solution)/shard_map/concatenate | solution.py:425
  0.8 0.7 %collective-permute-start.7 = (bf16[128,256]{1,0:T(8,128)(2,1)S(1)}, bf16[128,256]{1,0:T(8,128)(2,1)S(1)}, u32[]{:S(2)}, u32[]{:S(2)}) collective-permute-start(bf16[128,256]{1,0:T(8,128)(2,1)S(1)} %pad_maximum_fusion.1), channel_id=1, source_target_pairs={{0,16},{8,72},{16,32},{24,88},{32,48},{40,104},{48,0},{56,120},{64... | collective-permute-start | bytes 196616 | tf_op jit(solution)/shard_map/ppermute | solution.py:60
  1.4 0.7 %collective-permute-start.10 = (bf16[128,256]{1,0:T(8,128)(2,1)S(1)}, bf16[128,256]{1,0:T(8,128)(2,1)S(1)}, u32[]{:S(2)}, u32[]{:S(2)}) collective-permute-start(bf16[128,256]{1,0:T(8,128)(2,1)S(1)} %pad_maximum_fusion.1), channel_id=1, source_target_pairs={{0,48},{8,200},{16,0},{24,216},{32,16},{40,232},{48,32},{56,248},{... | collective-permute-start | bytes 196616 | tf_op jit(solution)/shard_map/ppermute | solution.py:60
  2.1 0.7 %collective-permute-start.9 = (bf16[128,256]{1,0:T(8,128)(2,1)S(1)}, bf16[128,256]{1,0:T(8,128)(2,1)S(1)}, u32[]{:S(2)}, u32[]{:S(2)}) collective-permute-start(bf16[128,256]{1,0:T(8,128)(2,1)S(1)} %pad_maximum_fusion.1), channel_id=1, source_target_pairs={{0,32},{8,136},{16,48},{24,152},{32,0},{40,168},{48,16},{56,184},{... | collective-permute-start | bytes 196616 | tf_op jit(solution)/shard_map/ppermute | solution.py:60
  2.8 0.0 collective-permute-done.7
  2.8 1.3 %collective-permute-start.8 = (bf16[128,256]{1,0:T(8,128)(2,1)S(1)}, bf16[128,256]{1,0:T(8,128)(2,1)S(1)}, u32[]{:S(2)}, u32[]{:S(2)}) collective-permute-start(bf16[128,256]{1,0:T(8,128)(2,1)S(1)} %pad_maximum_fusion.1), channel_id=1, source_target_pairs={{0,1},{2,3},{4,5},{6,7},{8,9},{10,11},{12,13},{14,15},{16,17},{18,... | collective-permute-start | bytes 196616 | tf_op jit(solution)/shard_map/ppermute | solution.py:60
  4.1 0.0 copy-start
  4.1 0.7 %copy-done = bf16[1,64,256]{2,1,0:T(8,128)(2,1)S(1)} copy-done((bf16[1,64,256]{2,1,0:T(8,128)(2,1)S(1)}, bf16[1,64,256]{2,1,0:T(8,128)(2,1)}, u32[]{:S(2)}) %copy-start) | copy-done | bytes 32792
  4.9 0.0 copy-start.1
  4.9 0.8 %copy-done.1 = bf16[1,64,256]{2,1,0:T(8,128)(2,1)S(1)} copy-done((bf16[1,64,256]{2,1,0:T(8,128)(2,1)S(1)}, bf16[1,64,256]{2,1,0:T(8,128)(2,1)}, u32[]{:S(2)}) %copy-start.1) | copy-done | bytes 32792
  5.6 0.0 copy-start.2
  5.6 1.6 %copy-done.2 = bf16[512,8,256]{2,1,0:T(8,128)(2,1)S(1)} copy-done((bf16[512,8,256]{2,1,0:T(8,128)(2,1)S(1)}, bf16[512,8,256]{2,1,0:T(8,128)(2,1)}, u32[]{:S(2)}) %copy-start.2) | copy-done | bytes 2097176
  7.2 0.0 copy-start.3
  7.2 1.6 %copy-done.3 = bf16[512,8,256]{2,1,0:T(8,128)(2,1)S(1)} copy-done((bf16[512,8,256]{2,1,0:T(8,128)(2,1)S(1)}, bf16[512,8,256]{2,1,0:T(8,128)(2,1)}, u32[]{:S(2)}) %copy-start.3) | copy-done | bytes 2097176
  8.8 0.0 copy-start.4
  8.8 0.7 %copy-done.4 = s32[1,512]{1,0:T(1,128)S(1)} copy-done((s32[1,512]{1,0:T(1,128)S(1)}, s32[1,512]{1,0:T(1,128)}, u32[]{:S(2)}) %copy-start.4) | copy-done | bytes 2072
  9.5 0.0 copy-start.5
  9.5 0.7 %copy-done.5 = s32[256,2]{0,1:T(2,128)S(1)} copy-done((s32[256,2]{0,1:T(2,128)S(1)}, s32[256,2]{0,1:T(2,128)}, u32[]{:S(2)}) %copy-start.5) | copy-done | bytes 2072
  10.2 0.0 copy-start.6
  10.2 0.7 %copy-done.6 = s32[1,16]{1,0:T(1,128)S(1)} copy-done((s32[1,16]{1,0:T(1,128)S(1)}, s32[1,16]{1,0:T(1,128)}, u32[]{:S(2)}) %copy-start.6) | copy-done | bytes 88
  10.8 0.0 copy-start.8
  10.8 8.5 %shard_map.84 = (f32[2,512,128]{2,1,0:T(8,128)S(1)}, f32[2,512,256]{2,1,0:T(8,128)S(1)}, bf16[2,512,256]{2,1,0:T(8,128)(2,1)S(1)}, bf16[512,128]{1,0:T(8,128)(2,1)S(1)}, bf16[512,64]{1,0:T(8,128)(2,1)S(1)}) custom-call(s32[1,16]{1,0:T(1,128)S(1)} %copy-done.6, s32[1,512]{1,0:T(1,128)S(1)} %copy-done.4, s32[2,256]{1,0:T(2,128)S(1)} %bitcast.18, ...), custom_call_target="tpu_custom_call" | custom-call | flops 4429185024 | bytes 4325376 | tf_op jit(solution)/shard_map/pallas_call | solution.py:344
  19.3 0.0 collective-permute-done.10
  19.3 0.0 collective-permute-done.9
  19.3 0.0 collective-permute-done.8
  19.3 0.0 copy-done.8
  19.3 21.4 %conditional.1 = (bf16[1,64,2048]{2,1,0:T(8,128)(2,1)S(1)}) conditional(s32[]{:T(128)} %convert_element_type.3, (bf16[512,64]{1,0:T(8,128)(2,1)S(1)}, bf16[128,256]{1,0:T(8,128)(2,1)S(1)}, bf16[512,128]{1,0:T(8,128)(2,1)S(1)}, bf16[2,512,256]{2,1,0:T(8,128)(2,1)S(1)}, f32[2,512,128]{2,1,0:T(8,128)S(1)}, ...), branch_computations={%region_0.0_spmd, %region_1.0_spmd} | conditional | flops 2147876864 | bytes 9961760 | solution.py:471
  19.4 0.3 branch_0_fun.2
  19.6 19.2 %all_to_all.4.arrived_ref = bf16[32,2,16,256]{3,2,1,0:T(8,128)(2,1)S(1)} all-to-all(bf16[32,2,16,256]{3,2,1,0:T(8,128)(2,1)S(1)} %branch_0_fun.2), channel_id=1, replica_groups=mesh['x'=4,'y'=4,'c'=2,'t'=4,'s'=2] {'x','y','c'}, dimensions={0} | all-to-all | bytes 1048576 | tf_op jit(solution)/shard_map/cond/branch_0_fun/all_to_all | solution.py:468
  38.8 1.7 %branch_0_fun.3 = bf16[64,2048]{1,0:T(8,128)(2,1)S(1)} custom-call(bf16[32,2,16,256]{3,2,1,0:T(8,128)(2,1)S(1)} %all_to_all.4.arrived_ref, bf16[512,128]{1,0:T(8,128)(2,1)S(1)} %get-tuple-element.33.bias_ref, bf16[2,512,256]{2,1,0:T(8,128)(2,1)S(1)} %get-tuple-element.34.qa_ref, f32[2,512,128]{2,1,0:T(8,128)S(1)} %get-tuple-element.35.m_in, ...), custom_call_target="tpu_custom_call" | custom-call | flops 536870912 | bytes 524288 | tf_op jit(solution)/shard_map/cond/branch_0_fun/pallas_call | solution.py:409
  40.8 0.0 copy-start.7
  40.8 0.7 %copy-done.7 = bf16[1,64,2048]{2,1,0:T(8,128)(2,1)} copy-done((bf16[1,64,2048]{2,1,0:T(8,128)(2,1)}, bf16[1,64,2048]{2,1,0:T(8,128)(2,1)S(1)}, u32[]{:S(2)}) %copy-start.7) | copy-done | bytes 262168
Async XLA Ops:
  0.8 2.0 %collective-permute-start.7 = (bf16[128,256]{1,0:T(8,128)(2,1)S(1)}, bf16[128,256]{1,0:T(8,128)(2,1)S(1)}, u32[]{:S(2)}, u32[]{:S(2)}) collective-permute-start(bf16[128,256]{1,0:T(8,128)(2,1)S(1)} %pad_maximum_fusion.1), channel_id=1, source_target_pairs={{0,16},{8,72},{16,32},{24,88},{32,48},{40,104},{48,0},{56,120},{64... | collective-permute-start | bytes 196616 | tf_op jit(solution)/shard_map/ppermute | solution.py:60
  1.4 17.9 %collective-permute-start.10 = (bf16[128,256]{1,0:T(8,128)(2,1)S(1)}, bf16[128,256]{1,0:T(8,128)(2,1)S(1)}, u32[]{:S(2)}, u32[]{:S(2)}) collective-permute-start(bf16[128,256]{1,0:T(8,128)(2,1)S(1)} %pad_maximum_fusion.1), channel_id=1, source_target_pairs={{0,48},{8,200},{16,0},{24,216},{32,16},{40,232},{48,32},{56,248},{... | collective-permute-start | bytes 196616 | tf_op jit(solution)/shard_map/ppermute | solution.py:60
  2.1 17.2 %collective-permute-start.9 = (bf16[128,256]{1,0:T(8,128)(2,1)S(1)}, bf16[128,256]{1,0:T(8,128)(2,1)S(1)}, u32[]{:S(2)}, u32[]{:S(2)}) collective-permute-start(bf16[128,256]{1,0:T(8,128)(2,1)S(1)} %pad_maximum_fusion.1), channel_id=1, source_target_pairs={{0,32},{8,136},{16,48},{24,152},{32,0},{40,168},{48,16},{56,184},{... | collective-permute-start | bytes 196616 | tf_op jit(solution)/shard_map/ppermute | solution.py:60
  2.8 16.5 %collective-permute-start.8 = (bf16[128,256]{1,0:T(8,128)(2,1)S(1)}, bf16[128,256]{1,0:T(8,128)(2,1)S(1)}, u32[]{:S(2)}, u32[]{:S(2)}) collective-permute-start(bf16[128,256]{1,0:T(8,128)(2,1)S(1)} %pad_maximum_fusion.1), channel_id=1, source_target_pairs={{0,1},{2,3},{4,5},{6,7},{8,9},{10,11},{12,13},{14,15},{16,17},{18,... | collective-permute-start | bytes 196616 | tf_op jit(solution)/shard_map/ppermute | solution.py:60
  4.1 0.8 %copy-start = (bf16[1,64,256]{2,1,0:T(8,128)(2,1)S(1)}, bf16[1,64,256]{2,1,0:T(8,128)(2,1)}, u32[]{:S(2)}) copy-start(bf16[1,64,256]{2,1,0:T(8,128)(2,1)} %param.11) | copy-start | bytes 98308
  4.9 0.8 %copy-start.1 = (bf16[1,64,256]{2,1,0:T(8,128)(2,1)S(1)}, bf16[1,64,256]{2,1,0:T(8,128)(2,1)}, u32[]{:S(2)}) copy-start(bf16[1,64,256]{2,1,0:T(8,128)(2,1)} %param.12) | copy-start | bytes 98308
  5.6 1.6 %copy-start.2 = (bf16[512,8,256]{2,1,0:T(8,128)(2,1)S(1)}, bf16[512,8,256]{2,1,0:T(8,128)(2,1)}, u32[]{:S(2)}) copy-start(bf16[512,8,256]{2,1,0:T(8,128)(2,1)} %param.16) | copy-start | bytes 6291460
  7.2 1.6 %copy-start.3 = (bf16[512,8,256]{2,1,0:T(8,128)(2,1)S(1)}, bf16[512,8,256]{2,1,0:T(8,128)(2,1)}, u32[]{:S(2)}) copy-start(bf16[512,8,256]{2,1,0:T(8,128)(2,1)} %param.17) | copy-start | bytes 6291460
  8.8 0.7 %copy-start.4 = (s32[1,512]{1,0:T(1,128)S(1)}, s32[1,512]{1,0:T(1,128)}, u32[]{:S(2)}) copy-start(s32[1,512]{1,0:T(1,128)} %table_hbm.1) | copy-start | bytes 6148
  9.5 0.7 %copy-start.5 = (s32[256,2]{0,1:T(2,128)S(1)}, s32[256,2]{0,1:T(2,128)}, u32[]{:S(2)}) copy-start(s32[256,2]{0,1:T(2,128)} %param.13) | copy-start | bytes 6148
  10.2 0.7 %copy-start.6 = (s32[1,16]{1,0:T(1,128)S(1)}, s32[1,16]{1,0:T(1,128)}, u32[]{:S(2)}) copy-start(s32[1,16]{1,0:T(1,128)} %len_hbm.1) | copy-start | bytes 196
  10.8 8.5 %copy-start.8 = (bf16[1,64,2048]{2,1,0:T(8,128)(2,1)S(1)}, bf16[1,64,2048]{2,1,0:T(8,128)(2,1)}, u32[]{:S(2)}) copy-start(bf16[1,64,2048]{2,1,0:T(8,128)(2,1)} %param.10) | copy-start | bytes 786436
  40.8 0.7 %copy-start.7 = (bf16[1,64,2048]{2,1,0:T(8,128)(2,1)}, bf16[1,64,2048]{2,1,0:T(8,128)(2,1)S(1)}, u32[]{:S(2)}) copy-start(bf16[1,64,2048]{2,1,0:T(8,128)(2,1)S(1)} %get-tuple-element.84) | copy-start | bytes 786436

commit v3 on v2

--- a/solution.py
+++ b/solution.py
@@ -31,6 +31,7 @@
 BIG = float(2**20)
 TO_LOG2 = HEAD_WIDTH**-0.5 * math.log2(math.e)
 SIDE = 4
+HOPS = (1, 3, 2)
 AXES = ("x", "y", "c", "t", "s")
 SIZES = {"x": 4, "y": 4, "c": 2, "t": 4, "s": 2}
 CTX = ("x", "y", "c")
@@ -45,7 +46,8 @@
     jax.ShapeDtypeStruct((KV_HEADS, QROWS, 2 * HEAD_WIDTH), F32),
 ]
 ASKED = jax.ShapeDtypeStruct((KV_HEADS, QROWS, 2 * HEAD_WIDTH), BF16)
-ANSWER = jax.ShapeDtypeStruct((ROWS, QUERY_WIDTH), BF16)
+PIECE = jax.ShapeDtypeStruct((2 * ROWS, WIDTH), BF16)
+ANSWER = pltpu.HBM((ROWS, QUERY_WIDTH), BF16)
 
 
 def moved(shard, axes, target):
@@ -66,6 +68,10 @@
         bytes_accessed=keys * WIDTH * 4,
         transcendentals=KV_HEADS * QROWS * keys,
     )
+
+
+def in_hbm(*arrays):
+    return [pltpu.with_memory_space_constraint(a, pltpu.HBM) for a in arrays]
 
 
 def iota(shape, axis):
@@ -215,7 +221,7 @@
     def kernel(*refs):
         prompt_kernel(pieces, first, last, *refs)
 
-    before = [q] if first else list(state)
+    before = in_hbm(q) if first else list(state)
     return pl.pallas_call(
         kernel,
         out_shape=ANSWER if last else STATE + [ASKED] * first,
@@ -225,6 +231,45 @@
         compiler_params=pltpu.CompilerParams(vmem_limit_bytes=VMEM_LIMIT),
         cost_estimate=cost(keys),
     )(*before, *arrays)
+
+
+def join_kernel(k_hbm, v_hbm, kv_ref, sems):
+    copies = [
+        pltpu.make_async_copy(part, kv_ref.at[pl.ds(i * ROWS, ROWS)], sems.at[i])
+        for i, part in enumerate((k_hbm, v_hbm))
+    ]
+    for copy in copies:
+        copy.start()
+    for copy in copies:
+        copy.wait()
+
+
+def join(keys, values):
+    return pl.pallas_call(
+        join_kernel,
+        out_shape=PIECE,
+        in_specs=[HBM] * 2,
+        out_specs=VMEM,
+        scratch_shapes=[pltpu.SemaphoreType.DMA((2,))],
+        compiler_params=pltpu.CompilerParams(vmem_limit_bytes=VMEM_LIMIT),
+    )(*in_hbm(keys, values))
+
+
+def stack_kernel(*refs):
+    *parts, block_ref, again_ref = refs
+    for i in range(SIDE):
+        block_ref[i] = parts[i][...] if parts else jnp.zeros(PIECE.shape, BF16)
+    again_ref[...] = block_ref[0]
+
+
+def stack(parts):
+    return pl.pallas_call(
+        stack_kernel,
+        out_shape=[jax.ShapeDtypeStruct((SIDE, *PIECE.shape), BF16), PIECE],
+        in_specs=[VMEM] * len(parts),
+        out_specs=[VMEM] * 2,
+        compiler_params=pltpu.CompilerParams(vmem_limit_bytes=VMEM_LIMIT),
+    )(*parts)
 
 
 def pool_kernel(
@@ -370,7 +415,7 @@
         ],
         compiler_params=pltpu.CompilerParams(vmem_limit_bytes=VMEM_LIMIT),
         cost_estimate=cost(TOKENS + NEW),
-    )(lengths, table, owners, q, new_k, new_v, cache_k, cache_v)
+    )(*in_hbm(lengths, table, owners, q, new_k, new_v, cache_k, cache_v))
 
 
 def pick_kernel(pick_ref, kv_ref, out_ref):
@@ -420,57 +465,57 @@
 def body(
     queries, keys, values, page_owner, lengths, page_table, group_cache_keys, group_cache_values
 ):
-    section = lax.axis_index("s")
+    first_section = lax.axis_index("s") == 0
     q = queries[0]
-    kv = jnp.concatenate([keys[0], values[0]], axis=0)
-
-    def first_hop(k):
-        def target(x, y, c, s):
-            if s == 1:
-                return None
-            return (x, y + k, c, s) if c == 0 else (x + k, y, c, s)
-
-        return moved(kv, ("x", "y", "c", "s"), target)
-
-    near = [first_hop(k) for k in (1, 3, 2)]
-    later_kv, near[0] = lax.optimization_barrier((kv, near[0]))
-    crossed = moved(later_kv, ("s",), lambda s: (1,) if s == 0 else None)
-    m, acc, qa, hand_bias, pick = pool_attend(
+
+    def shifted(part, k, swap):
+        def target(x, y, c):
+            return (x, y + k, c) if (c == 0) != swap else (x + k, y, c)
+
+        return moved(part, CTX, target)
+
+    def other_core(part):
+        return moved(part, ("c",), lambda c: (1 - c,))
+
+    def gather_near(keys, values):
+        kv = join(keys, values)
+        near = {k: shifted(kv, k, False) for k in HOPS}
+        return stack([kv] + [near[k] for k in (1, 2, 3)])
+
+    def wait_near(keys, values):
+        return stack([])
+
+    block, kv = lax.cond(first_section, gather_near, wait_near, keys[0], values[0])
+    crossed = moved(kv, ("s",), lambda s: (1,) if s == 0 else None)
+    ready = pool_attend(
         lengths, page_table, page_owner.T, q, keys[0], values[0],
         group_cache_keys.reshape(TOKENS, WIDTH), group_cache_values.reshape(TOKENS, WIDTH),
     )
 
-    def prompt(q, kv, near, crossed, *_):
-        block = jnp.stack([kv, near[0], near[2], near[1]])
-
-        def second_hop(k):
-            def target(x, y, c):
-                return (x + k, y, c) if c == 0 else (x, y + k, c)
-
-            return moved(block, CTX, target)
-
-        def other_core(piece):
-            return moved(piece, ("c",), lambda c: (1 - c,))
-
+    def prompt(q, block, crossed, *_):
         block_other = other_core(block)
-        hops = (1, 3, 2)
-        far = [second_hop(k) for k in hops]
+        h = HOPS
+        far = [shifted(block, k, True) for k in h]
         m, acc, qa = prompt_attend([block, block_other], [(False, 0), (True, 0)], q=q)
-        far, m, acc, qa = lax.optimization_barrier((far, m, acc, qa))
-        far_other = [other_core(piece) for piece in far]
-        m, acc = prompt_attend(far, [(False, k) for k in hops], state=(qa, m, acc))
+        far_other = []
+        for i in range(3):
+            far[i], m, acc = lax.optimization_barrier((far[i], m, acc))
+            far_other.append(other_core(far[i]))
+        m, acc = prompt_attend(
+            [far[0], far[1], far_other[0]], [(False, h[0]), (False, h[1]), (True, h[0])],
+            state=(qa, m, acc),
+        )
         return prompt_attend(
-            far_other, [(True, k) for k in hops], state=(qa, m, acc), last=True
+            [far[2], far_other[1], far_other[2]], [(False, h[2]), (True, h[1]), (True, h[2])],
+            state=(qa, m, acc), last=True,
         )
 
-    def decode(q, kv, near, crossed, m, acc, qa, hand_bias, pick):
+    def decode(q, block, crossed, m, acc, qa, hand_bias, pick):
         outgoing = pick_pages(pick, crossed)
         arrived = lax.all_to_all(outgoing, CTX, 0, 0, tiled=True)
         return hand_attend(arrived, hand_bias, qa, m, acc)
 
-    out = lax.cond(
-        section == 0, prompt, decode, q, kv, near, crossed, m, acc, qa, hand_bias, pick
-    )
+    out = lax.cond(first_section, prompt, decode, q, block, crossed, *ready)
     return out[None]
 
 

time: 42 us -> 36 us (0.86)
  local copies, waits for them, and re-layouts: 7.41 us -> 0 us
  starting transfers between devices: 3.27 us -> 1.29 us
  blocking collectives: 19.2 us -> 21 us
  waiting for transfers between devices: 0.01 us -> 1.27 us
  Pallas kernels: 10.5 us -> 11.7 us
  other arithmetic: 0.78 us -> 0 us
    unnamed x18 -> x0, local copies, waits for them, and re-layouts: 7.41 us -> none
    ppermute x4 -> x1, starting transfers between devices: 3.27 us -> 1.29 us  [moved(): return lax.ppermute(shard, axes if len(axes) > 1 else axes[0], pairs)]
    all_to_all x1, blocking collectives: 19.2 us -> 21 us  [decode(): arrived = lax.all_to_all(outgoing, CTX, 0, 0, tiled=True)]
    ppermute x4 -> x1, waiting for transfers between devices: 0.01 us -> 1.27 us  [moved(): return lax.ppermute(shard, axes if len(axes) > 1 else axes[0], pairs)]
    pallas_call x1, Pallas kernels: 8.47 us -> 9.55 us  [pool_attend(): pl.pallas_call(pool_kernel, out_shape=STATE + [ASKED, jax.ShapeDtypeStruc...]
    concatenate x1 -> x0, other arithmetic: 0.78 us -> none  [body(): kv = jnp.concatenate([keys[0], values[0]], axis=0)]
  transfers between devices with their start and end apart: 4 -> 1, of which waited for: 0 -> 1; matrix products, arithmetic and copies ran while one was open for 0% -> 0% of each run, Pallas kernels for 20% -> 27%
where the time goes in v3:
time: 36 us; the launch traced here: 35.7 us
  blocking collectives  21 us (58%)
  Pallas kernels  11.7 us (32%)
  starting transfers between devices  1.29 us (4%)
  waiting for transfers between devices  1.27 us (4%)
    all_to_all x1, blocking collectives, decode(): arrived = lax.all_to_all(outgoing, CTX, 0, 0, tiled=True)  21 us
    pallas_call x1, Pallas kernels, pool_attend(): pl.pallas_call(pool_kernel, out_shape=STATE + [ASKED, jax.ShapeDtypeStruc...  9.55 us
    pallas_call x1, Pallas kernels, hand_attend(): pl.pallas_call(hand_kernel, out_shape=ANSWER, in_specs=[VMEM] * 5, out_sp...  1.89 us
    ppermute x1, starting transfers between devices, moved(): return lax.ppermute(shard, axes if len(axes) > 1 else axes[0], pairs)  1.29 us
    ppermute x1, waiting for transfers between devices, moved(): return lax.ppermute(shard, axes if len(axes) > 1 else axes[0], pairs)  1.27 us
  transfers between devices with their start and end apart: 1, of which 1 were waited for; matrix products, arithmetic and copies ran while one was open for 0% of the time, Pallas kernels for 27%

profile of v3, /device:TPU:225, one launch (start us, length us, event | category | flops | bytes accessed | tf_op | source)
XLA Modules:
  0.0 35.7 jit_solution(16399440536801247103)
XLA Ops:
  0.0 1.3 %collective-permute-start.10 = (bf16[128,256]{1,0:T(8,128)(2,1)S(1)}, bf16[128,256]{1,0:T(8,128)(2,1)S(1)}, u32[]{:S(2)}, u32[]{:S(2)}) collective-permute-start(bf16[128,256]{1,0:T(8,128)(2,1)S(1)} %get-tuple-element.61), channel_id=1, source_target_pairs={{0,1},{2,3},{4,5},{6,7},{8,9},{10,11},{12,13},{14,15},{16,17},{18,... | collective-permute-start | bytes 196616 | tf_op jit(solution)/shard_map/ppermute | solution.py:62
  1.3 9.6 %shard_map.84 = (f32[2,512,128]{2,1,0:T(8,128)S(1)}, f32[2,512,256]{2,1,0:T(8,128)S(1)}, bf16[2,512,256]{2,1,0:T(8,128)(2,1)S(1)}, bf16[512,128]{1,0:T(8,128)(2,1)S(1)}, bf16[512,64]{1,0:T(8,128)(2,1)S(1)}) custom-call(s32[1,16]{1,0:T(1,128)} %len_hbm.1, s32[1,512]{1,0:T(1,128)} %table_hbm.1, s32[2,256]{1,0:T(2,128)} %bitcast.18, bf16[64,2048]{1,0:T(8,128)(2,1)} %bitcast.16, ...), custom_call_target="tpu_custom_call" | custom-call | flops 4429185024 | bytes 4325376 | tf_op jit(solution)/shard_map/pallas_call | solution.py:389
  10.9 1.3 %collective-permute-done.10 = bf16[128,256]{1,0:T(8,128)(2,1)S(1)} collective-permute-done((bf16[128,256]{1,0:T(8,128)(2,1)S(1)}, bf16[128,256]{1,0:T(8,128)(2,1)S(1)}, u32[]{:S(2)}, u32[]{:S(2)}) %collective-permute-start.10) | collective-permute-done | bytes 65568 | tf_op jit(solution)/shard_map/ppermute | solution.py:62
  12.2 23.4 %conditional.3 = (bf16[1,64,2048]{2,1,0:T(8,128)(2,1)}) conditional(s32[]{:T(128)} %convert_element_type.4, (bf16[512,64]{1,0:T(8,128)(2,1)S(1)}, bf16[128,256]{1,0:T(8,128)(2,1)S(1)}, bf16[512,128]{1,0:T(8,128)(2,1)S(1)}, bf16[2,512,256]{2,1,0:T(8,128)(2,1)S(1)}, f32[2,512,128]{2,1,0:T(8,128)S(1)}, ...), branch_computations={%region_2.0_spmd, %region_3.0_spmd} | conditional | flops 2147483648 | bytes 9437472 | solution.py:518
  12.2 0.3 branch_0_fun.4
  12.5 21.0 %all_to_all.4.arrived_ref = bf16[32,2,16,256]{3,2,1,0:T(8,128)(2,1)S(1)} all-to-all(bf16[32,2,16,256]{3,2,1,0:T(8,128)(2,1)S(1)} %branch_0_fun.4), channel_id=1, replica_groups=mesh['x'=4,'y'=4,'c'=2,'t'=4,'s'=2] {'x','y','c'}, dimensions={0} | all-to-all | bytes 1048576 | tf_op jit(solution)/shard_map/cond/branch_0_fun/all_to_all | solution.py:515
  33.4 1.9 %branch_0_fun.5 = bf16[64,2048]{1,0:T(8,128)(2,1)} custom-call(bf16[32,2,16,256]{3,2,1,0:T(8,128)(2,1)S(1)} %all_to_all.4.arrived_ref, bf16[512,128]{1,0:T(8,128)(2,1)S(1)} %get-tuple-element.33.bias_ref, bf16[2,512,256]{2,1,0:T(8,128)(2,1)S(1)} %get-tuple-element.34.qa_ref, f32[2,512,128]{2,1,0:T(8,128)S(1)} %get-tuple-element.35.m_in, ...), custom_call_target="tpu_custom_call" | custom-call | flops 536870912 | bytes 524288 | tf_op jit(solution)/shard_map/cond/branch_0_fun/pallas_call | solution.py:454
  (2 shorter events, 0.0 us)
Async XLA Ops:
  0.0 12.1 %collective-permute-start.10 = (bf16[128,256]{1,0:T(8,128)(2,1)S(1)}, bf16[128,256]{1,0:T(8,128)(2,1)S(1)}, u32[]{:S(2)}, u32[]{:S(2)}) collective-permute-start(bf16[128,256]{1,0:T(8,128)(2,1)S(1)} %get-tuple-element.61), channel_id=1, source_target_pairs={{0,1},{2,3},{4,5},{6,7},{8,9},{10,11},{12,13},{14,15},{16,17},{18,... | collective-permute-start | bytes 196616 | tf_op jit(solution)/shard_map/ppermute | solution.py:62

commit v4 on v3

--- a/solution.py
+++ b/solution.py
@@ -35,7 +35,8 @@
 AXES = ("x", "y", "c", "t", "s")
 SIZES = {"x": 4, "y": 4, "c": 2, "t": 4, "s": 2}
 CTX = ("x", "y", "c")
-VMEM_LIMIT = 40 * 1024 * 1024
+VMEM_LIMIT = 16 * 1024 * 1024
+POOL_LIMIT = 24 * 1024 * 1024
 F32 = jnp.float32
 BF16 = jnp.bfloat16
 I32 = jnp.int32
@@ -255,21 +256,41 @@
     )(*in_hbm(keys, values))
 
 
-def stack_kernel(*refs):
-    *parts, block_ref, again_ref = refs
-    for i in range(SIDE):
-        block_ref[i] = parts[i][...] if parts else jnp.zeros(PIECE.shape, BF16)
-    again_ref[...] = block_ref[0]
-
-
-def stack(parts):
-    return pl.pallas_call(
-        stack_kernel,
-        out_shape=[jax.ShapeDtypeStruct((SIDE, *PIECE.shape), BF16), PIECE],
+BLOCK = jax.ShapeDtypeStruct((SIDE, *PIECE.shape), BF16)
+
+
+def place_kernel(count, *refs):
+    parts, outs = refs[:count], refs[count:]
+    slots = [out.at[i] for out in outs for i in range(out.shape[0])]
+    for i, slot in enumerate(slots):
+        slot[...] = parts[i][...] if parts else jnp.zeros(slot.shape, BF16)
+
+
+def place(parts, counts):
+    def kernel(*refs):
+        place_kernel(len(parts), *refs)
+
+    return pl.pallas_call(
+        kernel,
+        out_shape=[pltpu.VMEM((n, *PIECE.shape), BF16) for n in counts],
         in_specs=[VMEM] * len(parts),
-        out_specs=[VMEM] * 2,
+        out_specs=[VMEM] * len(counts),
         compiler_params=pltpu.CompilerParams(vmem_limit_bytes=VMEM_LIMIT),
     )(*parts)
+
+
+def after_kernel(part_ref, state_ref, out_ref):
+    out_ref[...] = part_ref[...]
+
+
+def after(part, state):
+    return pl.pallas_call(
+        after_kernel,
+        out_shape=pltpu.VMEM(part.shape, part.dtype),
+        in_specs=[VMEM, VMEM],
+        out_specs=VMEM,
+        compiler_params=pltpu.CompilerParams(vmem_limit_bytes=VMEM_LIMIT),
+    )(part, state)
 
 
 def pool_kernel(
@@ -413,7 +434,7 @@
             pltpu.SemaphoreType.DMA((8,)),
             pltpu.SemaphoreType.DMA((KV_HEADS * GROUP_WIDTH,)),
         ],
-        compiler_params=pltpu.CompilerParams(vmem_limit_bytes=VMEM_LIMIT),
+        compiler_params=pltpu.CompilerParams(vmem_limit_bytes=POOL_LIMIT),
         cost_estimate=cost(TOKENS + NEW),
     )(*in_hbm(lengths, table, owners, q, new_k, new_v, cache_k, cache_v))
 
@@ -477,16 +498,20 @@
     def other_core(part):
         return moved(part, ("c",), lambda c: (1 - c,))
 
-    def gather_near(keys, values):
+    def next_ones(keys, values):
         kv = join(keys, values)
-        near = {k: shifted(kv, k, False) for k in HOPS}
-        return stack([kv] + [near[k] for k in (1, 2, 3)])
-
-    def wait_near(keys, values):
-        return stack([])
-
-    block, kv = lax.cond(first_section, gather_near, wait_near, keys[0], values[0])
-    crossed = moved(kv, ("s",), lambda s: (1,) if s == 0 else None)
+        return tuple(place([kv, kv, shifted(kv, 1, False), shifted(kv, 3, False)], [1, 3]))
+
+    kv, three = lax.cond(
+        first_section, next_ones, lambda *_: tuple(place([], [1, 3])), keys[0], values[0]
+    )
+    crossed = moved(kv[0], ("s",), lambda s: (1,) if s == 0 else None)
+
+    def the_last(three):
+        kv, near, back = three[0], three[1], three[2]
+        return place([kv, near, shifted(kv, 2, False), back], [SIDE])[0]
+
+    block = lax.cond(first_section, the_last, lambda *_: place([], [SIDE])[0], three)
     ready = pool_attend(
         lengths, page_table, page_owner.T, q, keys[0], values[0],
         group_cache_keys.reshape(TOKENS, WIDTH), group_cache_values.reshape(TOKENS, WIDTH),
@@ -498,17 +523,19 @@
         far = [shifted(block, k, True) for k in h]
         m, acc, qa = prompt_attend([block, block_other], [(False, 0), (True, 0)], q=q)
         far_other = []
-        for i in range(3):
+        for i in range(2):
             far[i], m, acc = lax.optimization_barrier((far[i], m, acc))
             far_other.append(other_core(far[i]))
         m, acc = prompt_attend(
             [far[0], far[1], far_other[0]], [(False, h[0]), (False, h[1]), (True, h[0])],
             state=(qa, m, acc),
         )
-        return prompt_attend(
-            [far[2], far_other[1], far_other[2]], [(False, h[2]), (True, h[1]), (True, h[2])],
-            state=(qa, m, acc), last=True,
+        last = far[2]
+        far_other.append(other_core(last))
+        m, acc = prompt_attend(
+            [far_other[1], last], [(True, h[1]), (False, h[2])], state=(qa, m, acc)
         )
+        return prompt_attend([far_other[2]], [(True, h[2])], state=(qa, m, acc), last=True)
 
     def decode(q, block, crossed, m, acc, qa, hand_bias, pick):
         outgoing = pick_pages(pick, crossed)

time: 36 us -> 33.5 us (0.931)
  blocking collectives: 21 us -> 19.6 us
  waiting for transfers between devices: 1.27 us -> 0.01 us
    all_to_all x1, blocking collectives: 21 us -> 19.6 us  [decode(): arrived = lax.all_to_all(outgoing, CTX, 0, 0, tiled=True)]
    ppermute x1, waiting for transfers between devices: 1.27 us -> 0.01 us  [moved(): return lax.ppermute(shard, axes if len(axes) > 1 else axes[0], pairs)]
  transfers between devices with their start and end apart: 1 -> 1, of which waited for: 1 -> 0; matrix products, arithmetic and copies ran while one was open for 0% -> 0% of each run, Pallas kernels for 27% -> 29%
where the time goes in v4:
time: 33.5 us; the launch traced here: 33.2 us
  blocking collectives  19.6 us (59%)
  Pallas kernels  11.8 us (35%)
  starting transfers between devices  1.29 us (4%)
    all_to_all x1, blocking collectives, decode(): arrived = lax.all_to_all(outgoing, CTX, 0, 0, tiled=True)  19.6 us
    pallas_call x1, Pallas kernels, pool_attend(): pl.pallas_call(pool_kernel, out_shape=STATE + [ASKED, jax.ShapeDtypeStruc...  9.56 us
    pallas_call x1, Pallas kernels, hand_attend(): pl.pallas_call(hand_kernel, out_shape=ANSWER, in_specs=[VMEM] * 5, out_sp...  1.89 us
    ppermute x1, starting transfers between devices, moved(): return lax.ppermute(shard, axes if len(axes) > 1 else axes[0], pairs)  1.29 us
  transfers between devices with their start and end apart: 1, of which 0 were waited for; matrix products, arithmetic and copies ran while one was open for 0% of the time, Pallas kernels for 29%

profile of v4, /device:TPU:225, one launch (start us, length us, event | category | flops | bytes accessed | tf_op | source)
XLA Modules:
  0.0 33.2 jit_solution(12278874639399387576)
XLA Ops:
  0.0 1.3 %collective-permute-start.10 = (bf16[128,256]{1,0:T(8,128)(2,1)S(1)}, bf16[128,256]{1,0:T(8,128)(2,1)S(1)}, u32[]{:S(2)}, u32[]{:S(2)}) collective-permute-start(bf16[128,256]{1,0:T(8,128)(2,1)S(1)} %bitcast.15), channel_id=1, source_target_pairs={{0,1},{2,3},{4,5},{6,7},{8,9},{10,11},{12,13},{14,15},{16,17},{18,... | collective-permute-start | bytes 196616 | tf_op jit(solution)/shard_map/ppermute | solution.py:63
  1.3 9.6 %shard_map.84 = (f32[2,512,128]{2,1,0:T(8,128)S(1)}, f32[2,512,256]{2,1,0:T(8,128)S(1)}, bf16[2,512,256]{2,1,0:T(8,128)(2,1)S(1)}, bf16[512,128]{1,0:T(8,128)(2,1)S(1)}, bf16[512,64]{1,0:T(8,128)(2,1)S(1)}) custom-call(s32[1,16]{1,0:T(1,128)} %len_hbm.1, s32[1,512]{1,0:T(1,128)} %table_hbm.1, s32[2,256]{1,0:T(2,128)} %bitcast.26, bf16[64,2048]{1,0:T(8,128)(2,1)} %bitcast.24, ...), custom_call_target="tpu_custom_call" | custom-call | flops 4429185024 | bytes 4325376 | tf_op jit(solution)/shard_map/pallas_call | solution.py:410
  10.9 0.0 collective-permute-done.10
  11.0 22.0 %conditional.5 = (bf16[1,64,2048]{2,1,0:T(8,128)(2,1)}) conditional(s32[]{:T(128)} %convert_element_type.2, (bf16[512,64]{1,0:T(8,128)(2,1)S(1)}, bf16[128,256]{1,0:T(8,128)(2,1)S(1)}, bf16[512,128]{1,0:T(8,128)(2,1)S(1)}, bf16[2,512,256]{2,1,0:T(8,128)(2,1)S(1)}, f32[2,512,128]{2,1,0:T(8,128)S(1)}, ...), branch_computations={%region_4.0_spmd, %region_5.0_spmd} | conditional | flops 2147483648 | bytes 9437472 | solution.py:545
  11.0 0.3 branch_0_fun.6
  11.2 19.6 %all_to_all.4.arrived_ref = bf16[32,2,16,256]{3,2,1,0:T(8,128)(2,1)S(1)} all-to-all(bf16[32,2,16,256]{3,2,1,0:T(8,128)(2,1)S(1)} %branch_0_fun.6), channel_id=1, replica_groups=mesh['x'=4,'y'=4,'c'=2,'t'=4,'s'=2] {'x','y','c'}, dimensions={0} | all-to-all | bytes 1048576 | tf_op jit(solution)/shard_map/cond/branch_0_fun/all_to_all | solution.py:542
  30.9 1.9 %branch_0_fun.7 = bf16[64,2048]{1,0:T(8,128)(2,1)} custom-call(bf16[32,2,16,256]{3,2,1,0:T(8,128)(2,1)S(1)} %all_to_all.4.arrived_ref, bf16[512,128]{1,0:T(8,128)(2,1)S(1)} %get-tuple-element.42.bias_ref, bf16[2,512,256]{2,1,0:T(8,128)(2,1)S(1)} %get-tuple-element.43.qa_ref, f32[2,512,128]{2,1,0:T(8,128)S(1)} %get-tuple-element.44.m_in, ...), custom_call_target="tpu_custom_call" | custom-call | flops 536870912 | bytes 524288 | tf_op jit(solution)/shard_map/cond/branch_0_fun/pallas_call | solution.py:475
  (4 shorter events, 0.1 us)
Async XLA Ops:
  0.0 10.9 %collective-permute-start.10 = (bf16[128,256]{1,0:T(8,128)(2,1)S(1)}, bf16[128,256]{1,0:T(8,128)(2,1)S(1)}, u32[]{:S(2)}, u32[]{:S(2)}) collective-permute-start(bf16[128,256]{1,0:T(8,128)(2,1)S(1)} %bitcast.15), channel_id=1, source_target_pairs={{0,1},{2,3},{4,5},{6,7},{8,9},{10,11},{12,13},{14,15},{16,17},{18,... | collective-permute-start | bytes 196616 | tf_op jit(solution)/shard_map/ppermute | solution.py:63

commit v5 on v4

--- a/solution.py
+++ b/solution.py
@@ -27,6 +27,7 @@
 TOKENS = PAGES * PAGE_TOKENS
 HAND_TOKENS = HAND * PAGE_TOKENS
 CHUNK = 512
+HALF_CHUNKS = TOKENS // CHUNK // 2
 NEW = 128
 BIG = float(2**20)
 TO_LOG2 = HEAD_WIDTH**-0.5 * math.log2(math.e)
@@ -297,7 +298,7 @@
     len_hbm, table_hbm, owner_hbm, q_hbm, new_k_hbm, new_v_hbm, k_hbm, v_hbm,
     m_ref, acc_ref, qa_ref, hand_bias_ref, pick_ref,
     k_ref, v_ref, new_k_ref, new_v_ref, bias_ref, new_bias_ref, s_ref, new_s_ref, mx_ref,
-    len_ref, table_ref, owner_ref, own_ref, sems, ask_sems,
+    len_ref, table_ref, owner_ref, own_ref, sems, cache_sems, ask_sems,
 ):
     @pl.when(lax.axis_index("s") == 1)
     def _():
@@ -310,10 +311,15 @@
         large = ask(q_hbm, qa_ref, ask_sems) + [
             pltpu.make_async_copy(new_k_hbm, new_k_ref.at[pl.ds(0, ROWS)], sems.at[4]),
             pltpu.make_async_copy(new_v_hbm, new_v_ref.at[pl.ds(0, ROWS)], sems.at[5]),
-            pltpu.make_async_copy(k_hbm, k_ref, sems.at[6]),
-            pltpu.make_async_copy(v_hbm, v_ref, sems.at[7]),
         ]
-        for copy in small + large:
+        half = TOKENS // 2
+
+        def cache_half(i, part):
+            source, goal = ((k_hbm, k_ref), (v_hbm, v_ref))[i]
+            rows = pl.ds(pl.multiple_of(part * half, half), half)
+            return pltpu.make_async_copy(source.at[rows], goal.at[rows], cache_sems.at[i, part])
+
+        for copy in small + large + [cache_half(i, part) for i in range(2) for part in range(2)]:
             copy.start()
         me = lax.axis_index("x") * 8 + lax.axis_index("y") * 2 + lax.axis_index("c")
         mark_rows(qa_ref)
@@ -384,23 +390,35 @@
             new_s_ref[...] = s
             mx_ref[...] = s
 
-            def scores(c, carry):
-                s = score(qa_ref[j], k_ref[rows(c), lanes(j)], bias_ref[rows(c)])
-                s_ref[c] = s
-                mx_ref[...] = jnp.maximum(mx_ref[...], peak(s))
+            def scores(part, carry):
+                @pl.when(j == 0)
+                def _():
+                    cache_half(0, part).wait()
+
+                for i in range(HALF_CHUNKS):
+                    c = part * HALF_CHUNKS + i
+                    s = score(qa_ref[j], k_ref[rows(c), lanes(j)], bias_ref[rows(c)])
+                    s_ref[c] = s
+                    mx_ref[...] = jnp.maximum(mx_ref[...], peak(s))
                 return carry
 
-            lax.fori_loop(0, TOKENS // CHUNK, scores, 0, unroll=4)
+            lax.fori_loop(0, 2, scores, 0)
             top = spread(mx_ref[...])
             m_ref[j] = top
             mx_ref[...] = top * TO_LOG2
             acc_ref[j] = mix(new_s_ref[...], mx_ref[...], new_v_ref[:, lanes(j)])
 
-            def mixes(c, carry):
-                acc_ref[j] += mix(s_ref[c], mx_ref[...], v_ref[rows(c), lanes(j)])
+            def mixes(part, carry):
+                @pl.when(j == 0)
+                def _():
+                    cache_half(1, part).wait()
+
+                for i in range(HALF_CHUNKS):
+                    c = part * HALF_CHUNKS + i
+                    acc_ref[j] += mix(s_ref[c], mx_ref[...], v_ref[rows(c), lanes(j)])
                 return carry
 
-            lax.fori_loop(0, TOKENS // CHUNK, mixes, 0, unroll=4)
+            lax.fori_loop(0, 2, mixes, 0)
             return carry
 
         lax.fori_loop(0, KV_HEADS, one_head, 0)
@@ -431,7 +449,8 @@
             pltpu.VMEM((1, PAGES), I32),
             pltpu.VMEM((TOP, PROMPT_PAGES), I32),
             pltpu.SMEM((TOP, PROMPT_PAGES), I32),
-            pltpu.SemaphoreType.DMA((8,)),
+            pltpu.SemaphoreType.DMA((6,)),
+            pltpu.SemaphoreType.DMA((2, 2)),
             pltpu.SemaphoreType.DMA((KV_HEADS * GROUP_WIDTH,)),
         ],
         compiler_params=pltpu.CompilerParams(vmem_limit_bytes=POOL_LIMIT),
@@ -509,7 +528,7 @@
 
     def the_last(three):
         kv, near, back = three[0], three[1], three[2]
-        return place([kv, near, shifted(kv, 2, False), back], [SIDE])[0]
+        return place([kv, near, shifted(near, 1, False), back], [SIDE])[0]
 
     block = lax.cond(first_section, the_last, lambda *_: place([], [SIDE])[0], three)
     ready = pool_attend(

time: 33.5 us -> 33.4 us (level)
  Pallas kernels: 11.8 us -> 11 us
  blocking collectives: 19.6 us -> 20.4 us
    pallas_call x1, Pallas kernels: 9.56 us -> 8.77 us  [pool_attend(): pl.pallas_call(pool_kernel, out_shape=STATE + [ASKED, jax.ShapeDtypeStruc...]
    all_to_all x1, blocking collectives: 19.6 us -> 20.4 us  [decode(): arrived = lax.all_to_all(outgoing, CTX, 0, 0, tiled=True)]
  transfers between devices with their start and end apart: 1 -> 1, of which waited for: 0 -> 0; matrix products, arithmetic and copies ran while one was open for 0% -> 0% of each run, Pallas kernels for 29% -> 26%
where the time goes in v5:
time: 33.4 us; the launch traced here: 33.2 us
  blocking collectives  20.4 us (61%)
  Pallas kernels  11 us (33%)
  starting transfers between devices  1.29 us (4%)
    all_to_all x1, blocking collectives, decode(): arrived = lax.all_to_all(outgoing, CTX, 0, 0, tiled=True)  20.4 us
    pallas_call x1, Pallas kernels, pool_attend(): pl.pallas_call(pool_kernel, out_shape=STATE + [ASKED, jax.ShapeDtypeStruc...  8.77 us
    pallas_call x1, Pallas kernels, hand_attend(): pl.pallas_call(hand_kernel, out_shape=ANSWER, in_specs=[VMEM] * 5, out_sp...  1.89 us
    ppermute x1, starting transfers between devices, moved(): return lax.ppermute(shard, axes if len(axes) > 1 else axes[0], pairs)  1.29 us
  transfers between devices with their start and end apart: 1, of which 0 were waited for; matrix products, arithmetic and copies ran while one was open for 0% of the time, Pallas kernels for 26%

profile of v5, /device:TPU:225, one launch (start us, length us, event | category | flops | bytes accessed | tf_op | source)
XLA Modules:
  0.0 33.2 jit_solution(8660970089711395717)
XLA Ops:
  0.0 1.3 %collective-permute-start.10 = (bf16[128,256]{1,0:T(8,128)(2,1)S(1)}, bf16[128,256]{1,0:T(8,128)(2,1)S(1)}, u32[]{:S(2)}, u32[]{:S(2)}) collective-permute-start(bf16[128,256]{1,0:T(8,128)(2,1)S(1)} %bitcast.15), channel_id=1, source_target_pairs={{0,1},{2,3},{4,5},{6,7},{8,9},{10,11},{12,13},{14,15},{16,17},{18,... | collective-permute-start | bytes 196616 | tf_op jit(solution)/shard_map/ppermute | solution.py:64
  1.3 8.8 %shard_map.84 = (f32[2,512,128]{2,1,0:T(8,128)S(1)}, f32[2,512,256]{2,1,0:T(8,128)S(1)}, bf16[2,512,256]{2,1,0:T(8,128)(2,1)S(1)}, bf16[512,128]{1,0:T(8,128)(2,1)S(1)}, bf16[512,64]{1,0:T(8,128)(2,1)S(1)}) custom-call(s32[1,16]{1,0:T(1,128)} %len_hbm.1, s32[1,512]{1,0:T(1,128)} %table_hbm.1, s32[2,256]{1,0:T(2,128)} %bitcast.26, bf16[64,2048]{1,0:T(8,128)(2,1)} %bitcast.24, ...), custom_call_target="tpu_custom_call" | custom-call | flops 4429185024 | bytes 4325376 | tf_op jit(solution)/shard_map/pallas_call | solution.py:428
  10.2 0.0 collective-permute-done.10
  10.2 22.8 %conditional.5 = (bf16[1,64,2048]{2,1,0:T(8,128)(2,1)}) conditional(s32[]{:T(128)} %convert_element_type.2, (bf16[512,64]{1,0:T(8,128)(2,1)S(1)}, bf16[128,256]{1,0:T(8,128)(2,1)S(1)}, bf16[512,128]{1,0:T(8,128)(2,1)S(1)}, bf16[2,512,256]{2,1,0:T(8,128)(2,1)S(1)}, f32[2,512,128]{2,1,0:T(8,128)S(1)}, ...), branch_computations={%region_4.0_spmd, %region_5.0_spmd} | conditional | flops 2147483648 | bytes 9437472 | solution.py:564
  10.2 0.3 branch_0_fun.6
  10.5 20.4 %all_to_all.4.arrived_ref = bf16[32,2,16,256]{3,2,1,0:T(8,128)(2,1)S(1)} all-to-all(bf16[32,2,16,256]{3,2,1,0:T(8,128)(2,1)S(1)} %branch_0_fun.6), channel_id=1, replica_groups=mesh['x'=4,'y'=4,'c'=2,'t'=4,'s'=2] {'x','y','c'}, dimensions={0} | all-to-all | bytes 1048576 | tf_op jit(solution)/shard_map/cond/branch_0_fun/all_to_all | solution.py:561
  30.9 1.9 %branch_0_fun.7 = bf16[64,2048]{1,0:T(8,128)(2,1)} custom-call(bf16[32,2,16,256]{3,2,1,0:T(8,128)(2,1)S(1)} %all_to_all.4.arrived_ref, bf16[512,128]{1,0:T(8,128)(2,1)S(1)} %get-tuple-element.42.bias_ref, bf16[2,512,256]{2,1,0:T(8,128)(2,1)S(1)} %get-tuple-element.43.qa_ref, f32[2,512,128]{2,1,0:T(8,128)S(1)} %get-tuple-element.44.m_in, ...), custom_call_target="tpu_custom_call" | custom-call | flops 536870912 | bytes 524288 | tf_op jit(solution)/shard_map/cond/branch_0_fun/pallas_call | solution.py:494
  (4 shorter events, 0.1 us)
Async XLA Ops:
  0.0 10.1 %collective-permute-start.10 = (bf16[128,256]{1,0:T(8,128)(2,1)S(1)}, bf16[128,256]{1,0:T(8,128)(2,1)S(1)}, u32[]{:S(2)}, u32[]{:S(2)}) collective-permute-start(bf16[128,256]{1,0:T(8,128)(2,1)S(1)} %bitcast.15), channel_id=1, source_target_pairs={{0,1},{2,3},{4,5},{6,7},{8,9},{10,11},{12,13},{14,15},{16,17},{18,... | collective-permute-start | bytes 196616 | tf_op jit(solution)/shard_map/ppermute | solution.py:64
